TPU v7x, 32 devices: a whole 2x2x4 slice. The times are simulated.
32 devices in a mesh: grp: 4 (over y, x), seq: 8 (over z, core).
Axes of the slice: x: 2, y: 2, z: 4, core: 2. Of those that a mesh axis runs over, the one named last changes fastest.
Arguments:
- layer_input: bfloat16 [8192, 1024], P(('grp', 'seq')), may hold values from -6 to 6
- segments: int32 [4, 2048], P('grp', 'seq'), may hold values from 0 to 2, never falling along the last dimension, each value on 1 to 2000 neighbouring positions
- ln_gain: bfloat16 [1024], P('seq'), may hold values from 0.5 to 1.5
- ln_bias: bfloat16 [1024], P('seq'), may hold values from -1.75 to 1.75
- w_value: bfloat16 [3072, 1024], P('seq'), may hold values from -0.1875 to 0.1875
- b_value: bfloat16 [3072], P('seq'), may hold values from -1.25 to 1.25
- w_reduce: bfloat16 [512, 1024], P('seq'), may hold values from -0.1875 to 0.1875
- b_reduce: bfloat16 [512], P('seq'), may hold values from -1.25 to 1.25
- lam_log: bfloat16 [512], P('seq'), may hold values from -2 to 0.5
- lam_freq: bfloat16 [512], P('seq'), may hold values from 0 to 50
- dss_w: bfloat16 [2, 512, 512], P(None, 'seq'), may hold values from -1.75 to 1.75
- log_step: bfloat16 [512], P('seq'), may hold values from -6.875 to -2.296875
- w_up: bfloat16 [3072, 512], P('seq'), may hold values from -0.5 to 0.5
- b_up: bfloat16 [3072], P('seq'), may hold values from -1.25 to 1.25
- w_out: bfloat16 [1024, 3072], P('seq'), may hold values from -0.21875 to 0.21875
- b_out: bfloat16 [1024], P('seq'), may hold values from -1.25 to 1.25
- out_cotangent: bfloat16 [8192, 1024], P(('grp', 'seq')), may hold values from -6 to 6
Outputs:
- layer_output: bfloat16 [8192, 1024], P(('grp', 'seq'))
- grad_input: float32 [8192, 1024], P(('grp', 'seq'))
- grad_ln_gain: float32 [1024], P('seq')
- grad_ln_bias: float32 [1024], P('seq')
- grad_w_value: float32 [3072, 1024], P('seq')
- grad_b_value: float32 [3072], P('seq')
- grad_w_reduce: float32 [512, 1024], P('seq')
- grad_b_reduce: float32 [512], P('seq')
- grad_lam_log: float32 [512], P('seq')
- grad_lam_freq: float32 [512], P('seq')
- grad_dss_w: float32 [2, 512, 512], P(None, 'seq')
- grad_log_step: float32 [512], P('seq')
- grad_w_up: float32 [3072, 512], P('seq')
- grad_b_up: float32 [3072], P('seq')
- grad_w_out: float32 [1024, 3072], P('seq')
- grad_b_out: float32 [1024], P('seq')
Inputs may be any that keep to these rules, and one draw needn't show every extreme that they name: `segments`: along each sequence the segment numbers never fall; every segment covers at most 2000 consecutive positions and one covers exactly 2000.
All inputs are finite; a program needn't handle non-finite values.
Results may differ from a plain program's by a relative error of at most 0.0077.
Values may be sent and summed in bfloat16 or wider, within the bound.
No kernel may reach another device: no remote copies, remote signals or barrier semaphores. Data moves between devices by JAX's collectives and lax.ppermute only.
A program may use at most 320 MiB of HBM per device.

v0:
```python
import functools

import jax
import jax.numpy as jnp
from jax import lax
from jax.experimental import pallas as pl
from jax.experimental.pallas import tpu as pltpu
from jax.sharding import PartitionSpec as P

f32, bf16 = jnp.float32, jnp.bfloat16
TILE = 128
MOST = 2000
LAGS = 2048
ROWS = 8
NT = (((1,), (1,)), ((), ()))
TN = (((0,), (0,)), ((), ()))


def params(mb=56):
    return pltpu.CompilerParams(vmem_limit_bytes=mb << 20)


def lag_blocks(length):
    return min(length // TILE, (MOST + TILE - 2) // TILE + 1)


def doc_count(length):
    return length // 1024 + 1


def cmul(a, b):
    return (a[0] * b[0] - a[1] * b[1], a[0] * b[1] + a[1] * b[0])


def mode_rates(lam_log_ref, lam_freq_ref, step_ref):
    lam_re = -jnp.exp(lam_log_ref[...])
    lam_im = lam_freq_ref[...]
    delta = jnp.exp(step_ref[...])
    return lam_re, lam_im, delta


def first_power(lam_re, lam_im, delta):
    growth = jnp.exp(delta * lam_re)
    phase = delta * lam_im
    return growth * jnp.cos(phase), growth * jnp.sin(phase)


def store_squares(one, sq_ref):
    cur = one
    for k in range(11):
        sq_ref[0, k], sq_ref[1, k] = cur
        if k < 10:
            cur = cmul(cur, cur)


def power_tiles(sq_ref, c, first, count):
    def sq(k):
        return sq_ref[0, k, pl.ds(c, 1), :], sq_ref[1, k, pl.ds(c, 1), :]

    width = sq_ref.shape[-1]
    row = lax.broadcasted_iota(jnp.int32, (8, width), 0)
    tile = None
    for k in range(3):
        re, im = sq(first + k)
        on = (row & (1 << k)) != 0
        term = jnp.where(on, re, 1.0), jnp.where(on, im, 0.0)
        tile = term if tile is None else cmul(tile, term)
    tiles, k = [tile], 3
    while len(tiles) < count:
        step = sq(first + k)
        tiles = tiles + [cmul(t, step) for t in tiles]
        k += 1
    return tiles


def split(x):
    hi = x.astype(bf16)
    return hi, (x - hi.astype(f32)).astype(bf16)


def store_fine(sq_ref, c, qh_ref, ql_ref):
    width = sq_ref.shape[-1]
    for t, pair in enumerate(power_tiles(sq_ref, c, 0, TILE // 8)):
        if t % 2 == 0:
            held = pair
            continue
        for part in range(2):
            hi, lo = split(jnp.concatenate([held[part], pair[part]], axis=0))
            qh_ref[8 * t - 8 : 8 * t + 8, part * width : (part + 1) * width] = hi
            ql_ref[8 * t - 8 : 8 * t + 8, part * width : (part + 1) * width] = lo


def taps_kernel(lam_log_ref, lam_freq_ref, w_ref, step_ref, tt_ref, sq_ref, cf_ref, qh_ref, ql_ref, p_ref):
    lam_re, lam_im, delta = mode_rates(lam_log_ref, lam_freq_ref, step_ref)
    one = first_power(lam_re, lam_im, delta)
    store_squares(one, sq_ref)
    modulus = lam_re * lam_re + lam_im * lam_im
    shift_re, shift_im = one[0] - 1.0, one[1]
    ratio = (
        (shift_re * lam_re + shift_im * lam_im) / modulus,
        (shift_im * lam_re - shift_re * lam_im) / modulus,
    )
    cf_ref[0], cf_ref[1] = cmul((w_ref[0], w_ref[1]), ratio)
    width = sq_ref.shape[-1]
    deep = tt_ref.shape[1]
    coarse = LAGS // TILE

    def channel(c, _):
        store_fine(sq_ref, c, qh_ref, ql_ref)
        coeff = cf_ref[0, pl.ds(c, 1), :], cf_ref[1, pl.ds(c, 1), :]
        tiles = [cmul(t, coeff) for t in power_tiles(sq_ref, c, 7, coarse // 8)]
        for part, sign in ((0, 1.0), (1, -1.0)):
            hi, lo = split(sign * jnp.concatenate([t[part] for t in tiles], axis=0))
            p_ref[:coarse, part * width : (part + 1) * width] = hi
            p_ref[coarse:, part * width : (part + 1) * width] = lo
        both = lax.dot_general(p_ref[...], qh_ref[...], NT, preferred_element_type=f32)
        low = lax.dot_general(p_ref[:coarse], ql_ref[...], NT, preferred_element_type=f32)
        taps = both[:coarse] + both[coarse:] + low
        empty = jnp.zeros((TILE, TILE), f32)
        pieces = [empty] + [
            jnp.broadcast_to(taps[d : d + 1], (TILE, TILE)) if d < coarse else empty for d in range(deep)
        ]
        skew = pltpu.roll(jnp.concatenate(pieces, axis=1), 0, 1, stride=1, stride_axis=0)
        for d in range(deep):
            tt_ref[c, d] = skew[:, (d + 1) * TILE : (d + 2) * TILE].astype(bf16)
        return 0

    lax.fori_loop(0, ROWS, channel, 0)


def make_toeplitz(lam_log, lam_freq, weights, log_step, deep):
    channels, modes = weights.shape[1:]
    return pl.pallas_call(
        taps_kernel,
        grid=(channels // ROWS,),
        in_specs=[
            pl.BlockSpec((1, modes), lambda i: (0, 0)),
            pl.BlockSpec((1, modes), lambda i: (0, 0)),
            pl.BlockSpec((2, ROWS, modes), lambda i: (0, i, 0)),
            pl.BlockSpec((ROWS, 1), lambda i: (i, 0)),
        ],
        out_specs=pl.BlockSpec((ROWS, deep, TILE, TILE), lambda i: (i, 0, 0, 0)),
        out_shape=jax.ShapeDtypeStruct((channels, deep, TILE, TILE), bf16),
        scratch_shapes=[
            pltpu.VMEM((2, 11, ROWS, modes), f32),
            pltpu.VMEM((2, ROWS, modes), f32),
            pltpu.VMEM((TILE, 2 * modes), bf16),
            pltpu.VMEM((TILE, 2 * modes), bf16),
            pltpu.VMEM((2 * LAGS // TILE, 2 * modes), bf16),
        ],
        compiler_params=params(),
    )(lam_log[None], lam_freq[None], weights, log_step[:, None])


def conv_kernel(docs, seg_ref, x_ref, tt_ref, y_ref, xs_ref, xw_ref):
    blocks, deep = x_ref.shape[1], tt_ref.shape[1]
    lead = deep - 1
    seg = seg_ref[...]
    for u in range(xs_ref.shape[0]):
        for k in range(docs):
            xs_ref[u, k, :lead, :] = jnp.zeros((lead, TILE), f32)

    def one(c, u):
        x = x_ref[c].astype(f32)
        for k in range(docs):
            xs_ref[u, k, lead:, :] = jnp.where(seg == k, x, 0.0)
        for k in range(docs):
            for d in range(deep):
                xw_ref[u, k * blocks : (k + 1) * blocks, d * TILE : (d + 1) * TILE] = xs_ref[
                    u, k, lead - d : lead - d + blocks, :
                ].astype(bf16)
        y = jnp.dot(xw_ref[u], tt_ref[c].reshape(deep * TILE, TILE), preferred_element_type=f32)
        out = jnp.zeros((blocks, TILE), f32)
        for k in range(docs):
            out = jnp.where(seg == k, y[k * blocks : (k + 1) * blocks], out)
        y_ref[c] = out.astype(bf16)

    def pair(i, _):
        for u in range(xs_ref.shape[0]):
            one(i * xs_ref.shape[0] + u, u)
        return 0

    lax.fori_loop(0, ROWS // xs_ref.shape[0], pair, 0)


def conv(seg, x, tt, unroll=2):
    channels, blocks, _ = x.shape
    deep = tt.shape[1]
    docs = doc_count(blocks * TILE)
    return pl.pallas_call(
        functools.partial(conv_kernel, docs),
        grid=(channels // ROWS,),
        in_specs=[
            pl.BlockSpec((blocks, TILE), lambda i: (0, 0)),
            pl.BlockSpec((ROWS, blocks, TILE), lambda i: (i, 0, 0)),
            pl.BlockSpec((ROWS, deep, TILE, TILE), lambda i: (i, 0, 0, 0)),
        ],
        out_specs=pl.BlockSpec((ROWS, blocks, TILE), lambda i: (i, 0, 0)),
        out_shape=jax.ShapeDtypeStruct(x.shape, bf16),
        scratch_shapes=[
            pltpu.VMEM((unroll, docs, blocks + deep - 1, TILE), f32),
            pltpu.VMEM((unroll, docs * blocks, deep * TILE), bf16),
        ],
        compiler_params=params(),
    )(seg, x, tt)


def back_kernel(docs, seg_ref, flip_ref, x_ref, g_ref, tt_ref, gx_ref, dt_ref, gs_ref, gw_ref, xst_ref):
    blocks, deep = x_ref.shape[1], tt_ref.shape[1]
    lead = deep - 1
    seg = seg_ref[...]
    for u in range(gs_ref.shape[0]):
        for k in range(docs):
            gs_ref[u, k, blocks:, :] = jnp.zeros((lead, TILE), f32)

    def one(c, u):
        g = g_ref[c].astype(f32)
        x = x_ref[c].astype(f32)
        for k in range(docs):
            gs_ref[u, k, :blocks, :] = jnp.where(seg == k, g, 0.0)
            xst_ref[u, k * blocks : (k + 1) * blocks, :] = jnp.where(seg == k, x, 0.0).astype(bf16)
        for k in range(docs):
            for d in range(deep):
                gw_ref[u, k * blocks : (k + 1) * blocks, d * TILE : (d + 1) * TILE] = gs_ref[
                    u, k, d : d + blocks, :
                ].astype(bf16)
        gx = jnp.zeros((docs * blocks, TILE), f32)
        for d in range(deep):
            gx += lax.dot_general(
                gw_ref[u, :, d * TILE : (d + 1) * TILE], tt_ref[c, d], NT, preferred_element_type=f32
            )
        out = jnp.zeros((blocks, TILE), f32)
        for k in range(docs):
            out = jnp.where(seg == k, gx[k * blocks : (k + 1) * blocks], out)
        gx_ref[c] = out.astype(bf16)
        xr = jnp.dot(xst_ref[u], flip_ref[...], preferred_element_type=f32).astype(bf16)
        wide = lax.dot_general(xr, gw_ref[u], TN, preferred_element_type=f32)
        wide = jnp.concatenate([wide, jnp.zeros((TILE, TILE), f32)], axis=1)
        flat = pltpu.roll(wide, wide.shape[1] - (TILE - 1), 1, stride=1, stride_axis=0)
        dt_ref[pl.ds(c, 1), :] = jnp.sum(flat[:, : LAGS], axis=0, keepdims=True)

    def pair(i, _):
        for u in range(gs_ref.shape[0]):
            one(i * gs_ref.shape[0] + u, u)
        return 0

    lax.fori_loop(0, ROWS // gs_ref.shape[0], pair, 0)


def conv_back(seg, x, g, tt, unroll=2):
    channels, blocks, _ = x.shape
    deep = tt.shape[1]
    docs = doc_count(blocks * TILE)
    flip = jnp.eye(TILE, dtype=bf16)[::-1]
    rows = pl.BlockSpec((ROWS, blocks, TILE), lambda i: (i, 0, 0))
    return pl.pallas_call(
        functools.partial(back_kernel, docs),
        grid=(channels // ROWS,),
        in_specs=[
            pl.BlockSpec((blocks, TILE), lambda i: (0, 0)),
            pl.BlockSpec((TILE, TILE), lambda i: (0, 0)),
            rows,
            rows,
            pl.BlockSpec((ROWS, deep, TILE, TILE), lambda i: (i, 0, 0, 0)),
        ],
        out_specs=[rows, pl.BlockSpec((ROWS, LAGS), lambda i: (i, 0))],
        out_shape=[jax.ShapeDtypeStruct(x.shape, bf16), jax.ShapeDtypeStruct((channels, LAGS), f32)],
        scratch_shapes=[
            pltpu.VMEM((unroll, docs, blocks + deep - 1, TILE), f32),
            pltpu.VMEM((unroll, docs * blocks, deep * TILE), bf16),
            pltpu.VMEM((unroll, docs * blocks, TILE), bf16),
        ],
        compiler_params=params(),
    )(seg, flip, x, g, tt)


def mode_grad_kernel(
    lam_log_ref, lam_freq_ref, w_ref, step_ref, dt_ref, gw_ref, gstep_ref, glam_ref, sq_ref, qh_ref, ql_ref, l_ref, s_ref
):
    lam_re, lam_im, delta = mode_rates(lam_log_ref, lam_freq_ref, step_ref)
    one = first_power(lam_re, lam_im, delta)
    store_squares(one, sq_ref)
    width = sq_ref.shape[-1]
    coarse = LAGS // TILE

    def channel(c, _):
        store_fine(sq_ref, c, qh_ref, ql_ref)
        dt = dt_ref[c]
        lane = lax.broadcasted_iota(jnp.int32, (coarse, TILE), 1).astype(f32)
        hi, lo = split(jnp.concatenate([dt, dt * lane], axis=0))
        l_ref[: 2 * coarse] = hi
        l_ref[2 * coarse :] = lo
        both = jnp.dot(l_ref[...], qh_ref[...], preferred_element_type=f32)
        low = jnp.dot(l_ref[: 2 * coarse], ql_ref[...], preferred_element_type=f32)
        v = both[: 2 * coarse] + both[2 * coarse :] + low
        tiles = power_tiles(sq_ref, c, 7, coarse // 8)
        power = tuple(jnp.concatenate([t[part] for t in tiles], axis=0) for part in range(2))
        v0 = v[:coarse, :width], v[:coarse, width:]
        row = lax.broadcasted_iota(jnp.int32, (coarse, width), 0).astype(f32) * float(TILE)
        v1 = tuple(row * v0[part] + v[coarse:, part * width : (part + 1) * width] for part in range(2))
        for n, pair in enumerate((v0, v1)):
            prod = cmul(power, pair)
            for part in range(2):
                s_ref[2 * n + part, pl.ds(c, 1), :] = jnp.sum(prod[part], axis=0, keepdims=True)
        return 0

    lax.fori_loop(0, ROWS, channel, 0)
    modulus = lam_re * lam_re + lam_im * lam_im
    inv = lam_re / modulus, -lam_im / modulus
    shift = one[0] - 1.0, one[1]
    ratio = cmul(shift, inv)
    w = w_ref[0], w_ref[1]
    s0 = s_ref[0], s_ref[1]
    s1 = s_ref[2], s_ref[3]
    coeff = cmul(w, ratio)
    gw = cmul(s0, ratio)
    gw_ref[0], gw_ref[1] = gw[0], -gw[1]
    near = cmul(s0, cmul(w, cmul(one, inv)))
    far = cmul(coeff, s1)
    z = near[0] + far[0], near[1] + far[1]
    back = cmul(s0, cmul(coeff, inv))
    big = delta * z[0] - back[0], delta * z[1] - back[1]
    step = jnp.sum((z[0] * lam_re - z[1] * lam_im) * delta, axis=1, keepdims=True)
    gstep_ref[...] = jnp.broadcast_to(step, gstep_ref.shape)

    @pl.when(pl.program_id(0) == 0)
    def _():
        glam_ref[...] = jnp.zeros(glam_ref.shape, f32)

    glam_ref[0] += big[0] * lam_re
    glam_ref[1] -= big[1]


def mode_grads(lam_log, lam_freq, weights, log_step, dt):
    channels, modes = weights.shape[1:]
    coarse = LAGS // TILE
    gw, gstep, glam = pl.pallas_call(
        mode_grad_kernel,
        grid=(channels // ROWS,),
        in_specs=[
            pl.BlockSpec((1, modes), lambda i: (0, 0)),
            pl.BlockSpec((1, modes), lambda i: (0, 0)),
            pl.BlockSpec((2, ROWS, modes), lambda i: (0, i, 0)),
            pl.BlockSpec((ROWS, 1), lambda i: (i, 0)),
            pl.BlockSpec((ROWS, coarse, TILE), lambda i: (i, 0, 0)),
        ],
        out_specs=[
            pl.BlockSpec((2, ROWS, modes), lambda i: (0, i, 0)),
            pl.BlockSpec((ROWS, TILE), lambda i: (i, 0)),
            pl.BlockSpec((2, ROWS, modes), lambda i: (0, 0, 0)),
        ],
        out_shape=[
            jax.ShapeDtypeStruct((2, channels, modes), f32),
            jax.ShapeDtypeStruct((channels, TILE), f32),
            jax.ShapeDtypeStruct((2, ROWS, modes), f32),
        ],
        scratch_shapes=[
            pltpu.VMEM((2, 11, ROWS, modes), f32),
            pltpu.VMEM((TILE, 2 * modes), bf16),
            pltpu.VMEM((TILE, 2 * modes), bf16),
            pltpu.VMEM((4 * coarse, TILE), bf16),
            pltpu.VMEM((4, ROWS, modes), f32),
        ],
        compiler_params=params(),
    )(lam_log[None], lam_freq[None], weights, log_step[:, None], dt.reshape(channels, coarse, TILE))
    return gw, gstep[:, 0], jnp.sum(glam, axis=1)


epsilon = 1e-05
contract_last = (((1,), (1,)), ((), ()))
contract_first = (((0,), (0,)), ((), ()))


def swap(x, k, n_grp):
    return x if k == 0 else lax.ppermute(x, "grp", [(i, i ^ k) for i in range(n_grp)])


def gather_grp(x, n_grp):
    return [swap(x, k, n_grp) for k in range(n_grp)]


def sum_scatter_grp(pieces, n_grp):
    total = pieces[0].astype(f32)
    for k in range(1, n_grp):
        total = total + swap(pieces[k].astype(bf16), k, n_grp).astype(f32)
    return total


def place_grp(x, n_grp, me, axis):
    held = jnp.stack(gather_grp(x, n_grp))
    order = jnp.arange(n_grp, dtype=jnp.int32) ^ me
    rows = [lax.dynamic_index_in_dim(held, order[j], 0, keepdims=False) for j in range(n_grp)]
    return jnp.stack(rows, axis=axis)


def body(
    n_grp,
    n_seq,
    layer_input,
    segments,
    ln_gain,
    ln_bias,
    w_value,
    b_value,
    w_reduce,
    b_reduce,
    lam_log,
    lam_freq,
    dss_w,
    log_step,
    w_up,
    b_up,
    w_out,
    b_out,
    out_cotangent,
):
    me = lax.axis_index("grp")
    tokens, wide = layer_input.shape
    part = w_value.shape[0] // n_grp
    quarter = n_seq * part
    reduced_width = w_reduce.shape[0] * n_seq

    small = (ln_gain, ln_bias, b_value, b_reduce, lam_log, lam_freq, b_up, b_out, segments[0].astype(bf16))
    packed = lax.all_gather(jnp.concatenate(small), "seq", axis=0)
    spots, fulls = 0, []
    for array in small:
        fulls.append(packed[:, spots : spots + array.shape[0]])
        spots += array.shape[0]
    gain_full, bias_full, value_bias, reduce_bias, decay_full, freq_full, up_bias, out_bias, doc_row = fulls
    gain_wide = gain_full.reshape(-1).astype(f32)
    bias_wide = bias_full.reshape(-1).astype(f32)
    value_bias = lax.dynamic_slice_in_dim(value_bias, me * part, part, 1).reshape(-1).astype(f32)
    up_bias = lax.dynamic_slice_in_dim(up_bias, me * part, part, 1).reshape(-1).astype(f32)

    reduce_full = lax.all_gather(w_reduce, "seq", axis=0, tiled=True)
    up_part = lax.all_gather(lax.dynamic_slice_in_dim(w_up, me * part, part, 0), "seq", axis=0, tiled=True)
    value_part = lax.all_gather(lax.dynamic_slice_in_dim(w_value, me * part, part, 0), "seq", axis=0, tiled=True)
    out_cols = lax.dynamic_index_in_dim(w_out.reshape(-1, n_seq, n_grp, part), me, 2, keepdims=False)
    out_part = lax.all_gather(out_cols.reshape(-1, quarter), "seq", axis=0, tiled=True)

    modes = (
        decay_full.reshape(-1).astype(f32),
        freq_full.reshape(-1).astype(f32),
        dss_w.astype(f32),
        log_step.astype(f32),
    )
    length = tokens * n_seq
    blocks = length // TILE
    toeplitz = make_toeplitz(*modes, lag_blocks(length))

    x_wide = layer_input.astype(f32)
    center = x_wide - jnp.mean(x_wide, axis=1, keepdims=True)
    inverse = lax.rsqrt(jnp.mean(center * center, axis=1, keepdims=True) + epsilon)
    unit = center * inverse
    normed = (unit * gain_wide + bias_wide).astype(bf16)

    normed_all = jnp.concatenate(gather_grp(normed, n_grp), axis=0)
    cot_all = jnp.concatenate(gather_grp(out_cotangent, n_grp), axis=0)

    pre_reduce = (
        lax.dot_general(reduce_full, normed, contract_last, preferred_element_type=f32)
        + reduce_bias.reshape(-1).astype(f32)[:, None]
    )
    reduced, reduce_pull = jax.vjp(jax.nn.gelu, pre_reduce)
    channel_in = lax.all_to_all(reduced.astype(bf16), "seq", split_axis=0, concat_axis=1, tiled=True)
    seg = doc_row.astype(jnp.int32).reshape(blocks, TILE)
    signal = channel_in.reshape(-1, blocks, TILE)
    channel_out = conv(seg, signal, toeplitz).reshape(-1, length)
    mixed = lax.all_to_all(channel_out, "seq", split_axis=1, concat_axis=0, tiled=True)
    mixed_all = jnp.concatenate(gather_grp(mixed, n_grp), axis=1)

    pre_value = lax.dot_general(normed_all, value_part, contract_last, preferred_element_type=f32) + value_bias
    activated, value_pull = jax.vjp(jax.nn.gelu, pre_value)
    g_gated = jnp.dot(cot_all, out_part, preferred_element_type=f32)
    pre_up = lax.dot_general(mixed_all, up_part, (((0,), (1,)), ((), ())), preferred_element_type=f32) + up_bias
    gated = (activated * pre_up).astype(bf16)
    g_activated = g_gated * pre_up
    g_pre_up = (g_gated * activated).astype(bf16)
    g_pre_value = value_pull(g_activated)[0].astype(bf16)

    g_mixed = lax.dot_general(up_part, g_pre_up, (((0,), (1,)), ((), ())), preferred_element_type=f32)
    g_mixed = sum_scatter_grp([g_mixed[:, k * tokens : (k + 1) * tokens] for k in range(n_grp)], n_grp)
    g_channel = lax.all_to_all(g_mixed.astype(bf16), "seq", split_axis=0, concat_axis=1, tiled=True)
    g_signal, g_taps = conv_back(seg, signal, g_channel.reshape(-1, blocks, TILE), toeplitz)
    g_reduced = lax.all_to_all(g_signal.reshape(-1, length), "seq", split_axis=1, concat_axis=0, tiled=True)
    g_weights, g_step, g_lam = mode_grads(*modes, g_taps)

    added = lax.dot_general(gated, out_part, contract_last, preferred_element_type=f32)
    added = sum_scatter_grp([added[k * tokens : (k + 1) * tokens] for k in range(n_grp)], n_grp)
    output = (x_wide + added + out_bias.reshape(-1).astype(f32)).astype(bf16)

    g_normed = jnp.dot(g_pre_value, value_part, preferred_element_type=f32)
    g_normed = sum_scatter_grp([g_normed[k * tokens : (k + 1) * tokens] for k in range(n_grp)], n_grp)

    def over_seq(x):
        return lax.psum_scatter(x.astype(bf16), "seq", scatter_dimension=0, tiled=True)

    g_out = over_seq(lax.dot_general(cot_all, gated, contract_first, preferred_element_type=f32))
    g_up = over_seq(lax.dot_general(g_pre_up, mixed_all, (((0,), (1,)), ((), ())), preferred_element_type=f32))
    g_value = over_seq(lax.dot_general(g_pre_value, normed_all, contract_first, preferred_element_type=f32))
    g_out = place_grp(g_out.reshape(-1, n_seq, part), n_grp, me, 2).reshape(w_out.shape).astype(f32)
    g_up = place_grp(g_up, n_grp, me, 0).reshape(w_up.shape).astype(f32)
    g_value = place_grp(g_value, n_grp, me, 0).reshape(w_value.shape).astype(f32)

    g_pre_reduce = reduce_pull(g_reduced.astype(f32))[0].astype(bf16)
    g_reduce = jnp.dot(g_pre_reduce, normed, preferred_element_type=f32)
    g_normed = g_normed + lax.dot_general(g_pre_reduce, reduce_full, contract_first, preferred_element_type=f32)
    g_unit = g_normed * gain_wide
    g_input = inverse * (
        g_unit
        - jnp.mean(g_unit, axis=1, keepdims=True)
        - unit * jnp.mean(g_unit * unit, axis=1, keepdims=True)
    ) + out_cotangent.astype(f32)

    def spread(x):
        return lax.dynamic_update_slice_in_dim(
            jnp.zeros((n_seq, n_grp, part), f32), x.reshape(n_seq, 1, part), me, 1
        ).reshape(n_seq, -1)

    vectors = (
        jnp.sum(g_normed * unit, axis=0).reshape(n_seq, -1),
        jnp.sum(g_normed, axis=0).reshape(n_seq, -1),
        spread(jnp.sum(g_pre_value.astype(f32), axis=0)),
        jnp.sum(g_pre_reduce.astype(f32), axis=1).reshape(n_seq, -1),
        g_lam[0].reshape(n_seq, -1),
        g_lam[1].reshape(n_seq, -1),
        spread(jnp.sum(g_pre_up.astype(f32), axis=0)),
        jnp.sum(out_cotangent.astype(f32), axis=0).reshape(n_seq, -1),
    )
    shard = lax.psum_scatter(jnp.concatenate(vectors, axis=1), "seq", scatter_dimension=0, tiled=False)
    g_reduce = lax.psum_scatter(g_reduce.astype(bf16), "seq", scatter_dimension=0, tiled=True)
    shard, g_step, g_weights, g_reduce = lax.psum(
        (shard, g_step, g_weights, g_reduce.astype(f32)), "grp"
    )
    sums, spots = [], 0
    for array in vectors:
        sums.append(shard[spots : spots + array.shape[1]])
        spots += array.shape[1]
    g_gain, g_bias, g_value_bias, g_reduce_bias, g_decay, g_freq, g_up_bias, g_out_bias = sums
    return (
        output,
        g_input,
        g_gain,
        g_bias,
        g_value,
        g_value_bias,
        g_reduce,
        g_reduce_bias,
        g_decay,
        g_freq,
        g_weights,
        g_step,
        g_up,
        g_up_bias,
        g_out,
        g_out_bias,
    )


def solution(mesh):
    by_token = P(("grp", "seq"), None)
    row, matrix, cube = P("seq"), P("seq", None), P(None, "seq", None)
    layer = (row, row, matrix, row, matrix, row, row, row, cube, row, matrix, row, matrix, row)
    return jax.shard_map(
        functools.partial(body, mesh.shape["grp"], mesh.shape["seq"]),
        mesh=mesh,
        in_specs=(by_token, P("grp", "seq"), *layer, by_token),
        out_specs=(by_token, by_token, *layer),
        check_vma=False,
    )
```

profile of v0, /device:TPU:0, one launch (start us, length us, event | category | flops | bytes accessed | tf_op | source)
XLA Modules:
  0.0 448.3 jit_solution(4700025413781083685)
XLA Ops:
  8.1 1.6 copy.55
  12.2 30.4 %all-reduce = bf16[12800]{0:T(1024)(128)(2,1)S(1)} all-reduce(bf16[12800]{0:T(1024)(128)(2,1)S(1)} %dynamic-update-slice), channel_id=2, replica_groups=mesh['grp'=4,'seq'=8] {'seq'}, use_global_device_ids=true, to_apply=%add | all-reduce | flops 12800 | bytes 51200
  43.6 1.6 collective-permute-start
  45.2 1.5 collective-permute-start.1
  47.7 2.5 collective-permute-start.11
  51.2 1.8 multiply_convert_fusion.2
  53.8 3.4 all-to-all-start
  60.6 37.9 %shard_map.288.tt_ref = bf16[64,16,128,128]{3,2,1,0:T(8,128)(2,1)} custom-call(f32[1,512]{1,0:T(1,128)} %reshape.230.lam_log_ref, f32[1,512]{1,0:T(1,128)} %reshape.231.lam_freq_ref, f32[2,64,512]{2,1,0:T(8,128)} %convert_element_type.235.w_ref, f32[64,1]{1,0:T(8,128)} %copy.53.step_ref), custom_call_target="tpu_custom_call" | custom-call | tf_op jit(solution)/shard_map/pallas_call | solution.py:133
  100.3 17.3 %shard_map.289 = bf16[64,16,128]{2,1,0:T(8,128)(2,1)} custom-call(s32[16,128]{1,0:T(8,128)} %reshape.228.seg_ref, bf16[64,16,128]{2,1,0:T(8,128)(2,1)} %reshape.210.x_ref, bf16[64,16,128,128]{3,2,1,0:T(8,128)(2,1)} %shard_map.288.tt_ref), custom_call_target="tpu_custom_call" | custom-call | tf_op jit(solution)/shard_map/pallas_call | solution.py:190
  117.6 1.0 all_to_all.51
  119.4 5.0 %all-to-all-start.1 = ((bf16[64,8,256]{2,0,1:T(8,128)(2,1)}), bf16[64,8,256]{2,0,1:T(8,128)(2,1)}, u32[]{:S(2)}, u32[]{:S(2)}) async-start(bf16[64,8,256]{2,0,1:T(8,128)(2,1)} %copy.54), calls=%async_computation.1 | async-start | bytes 524288 | tf_op jit(solution)/shard_map/all_to_all | solution.py:469
  125.6 18.8 %all_gather.22 = bf16[768,512]{1,0:T(8,128)(2,1)S(1)} all-gather(bf16[96,512]{1,0:T(8,128)(2,1)S(1)} %constant_dynamic-slice_fusion.10), channel_id=1, replica_groups=mesh['grp'=4,'seq'=8] {'seq'}, dimensions={0}, use_global_device_ids=true | all-gather | bytes 884736 | tf_op jit(solution)/shard_map/all_gather | solution.py:436
  144.9 1.9 constant_dynamic-update-slice_fusion.2
  146.8 1.4 collective-permute-start.2
  148.2 1.9 constant_dynamic-update-slice_fusion.1
  151.0 1.5 collective-permute-start.4
  152.5 1.3 collective-permute-done.3
  154.2 5.5 %fusion.65 = f32[1024,768]{1,0:T(8,128)} fusion(bf16[1024,1024]{1,0:T(8,128)(2,1)} %constant_dynamic-update-slice_fusion, bf16[1024,768]{0,1:T(8,128)(2,1)} %all-gather.9.cloned.1.call-done), kind=kOutput, calls=%fused_computation.138 | convolution fusion | flops 1610612736 | bytes 6815744 | tf_op jit(solution)/shard_map/dot_general | solution.py:474
  159.8 15.9 %collective-permute-done.4 = bf16[512,256]{1,0:T(8,128)(2,1)S(1)} collective-permute-done((bf16[512,256]{1,0:T(8,128)(2,1)}, bf16[512,256]{1,0:T(8,128)(2,1)S(1)}, u32[]{:S(2)}, u32[]{:S(2)}) %collective-permute-start.4) | collective-permute-done | bytes 262176 | tf_op jit(solution)/shard_map/ppermute | solution.py:375
  175.7 3.7 fusion.39
  179.4 9.2 %convert_reduce_fusion.1 = (f32[768]{0:T(1024)S(1)}, bf16[1024,768]{1,0:T(8,128)(2,1)}, bf16[1024,768]{1,0:T(8,128)(2,1)}, f32[768]{0:T(1024)S(1)}, bf16[1024,768]{1,0:T(8,128)(2,1)S(1)}) fusion(f32[768]{0:T(1024)S(1)} %reshape.226, f32[1024,768]{1,0:T(8,128)} %fusion.65, f32[1024,768]{1,0:T(8,128)} %fusion.39, f32[768]{0:T(1024)S(1)} %reshape.233, ...), kind=kOutput, calls=%fused_computation.10 | convolution fusion | flops 1644165632 | bytes 14692352 | tf_op jit(solution)/shard_map/dot_general | solution.py:472
  188.7 1.1 copy-done.4
  189.8 2.9 convolution_convert_fusion.3
  192.8 5.1 %convolution_convert_fusion = bf16[1024,768]{1,0:T(8,128)(2,1)} fusion(bf16[1024,1024]{1,0:T(8,128)(2,1)} %constant_dynamic-update-slice_fusion, bf16[1024,768]{1,0:T(8,128)(2,1)} %get-tuple-element.74), kind=kOutput, calls=%fused_computation.15 | convolution fusion | flops 1611399168 | bytes 5242880 | tf_op jit(solution)/shard_map/dot_general | solution.py:498
  198.2 4.8 %convolution_convert_fusion.1 = bf16[768,1024]{1,0:T(8,128)(2,1)} fusion(bf16[1024,768]{1,0:T(8,128)(2,1)} %get-tuple-element.72, bf16[256,1024]{1,0:T(8,128)(2,1)} %collective-permute-done.2, bf16[256,1024]{1,0:T(8,128)(2,1)} %collective-permute-done.1, bf16[256,1024]{1,0:T(8,128)(2,1)} %collective-permute-done, bf16[256,1024]{1,0:T(8,128)(2,1)S(1)} %fusion.15), kind=kOutput, calls=%fused_computation.16 | convolution fusion | flops 1619787776 | bytes 5242880 | tf_op jit(solution)/shard_map/dot_general | solution.py:500
  203.0 2.5 fusion.62
  206.1 1.6 collective-permute-start.16
  207.7 1.4 collective-permute-start.17
  209.1 5.7 %collective-permute-done.15 = bf16[512,256]{1,0:T(8,128)(2,1)S(1)} collective-permute-done((bf16[512,256]{1,0:T(8,128)(2,1)S(1)}, bf16[512,256]{1,0:T(8,128)(2,1)S(1)}, u32[]{:S(2)}, u32[]{:S(2)}) %collective-permute-start.15) | collective-permute-done | bytes 262176 | tf_op jit(solution)/shard_map/ppermute | solution.py:375
  214.8 4.0 collective-permute-done.16
  218.8 1.6 collective-permute-done.17
  221.2 3.4 all-to-all-start.2
  225.4 10.1 %all-to-all-done.2 = bf16[8,64,256]{2,1,0:T(8,128)(2,1)S(1)} async-done(((bf16[8,64,256]{2,1,0:T(8,128)(2,1)}), bf16[8,64,256]{2,1,0:T(8,128)(2,1)S(1)}, u32[]{:S(2)}, u32[]{:S(2)}) %all-to-all-start.2) | async-done | bytes 262176 | tf_op jit(solution)/shard_map/all_to_all | solution.py:483
  236.3 44.0 %shard_map.290 = (bf16[64,16,128]{2,1,0:T(8,128)(2,1)}, f32[64,2048]{1,0:T(8,128)}) custom-call(s32[16,128]{1,0:T(8,128)} %reshape.228.seg_ref, bf16[128,128]{1,0:T(8,128)(2,1)} %rev.3.flip_ref, bf16[64,16,128]{2,1,0:T(8,128)(2,1)} %reshape.210.x_ref, bf16[64,16,128]{2,1,0:T(8,128)(2,1)} %reshape.213.g_ref, bf16[64,16,128,128]{3,2,1,0:T(8,128)(2,1)} %shard_map.288.tt_ref), custom_call_target="tpu_custom_call" | custom-call | tf_op jit(solution)/shard_map/pallas_call | solution.py:256
  280.3 1.0 all_to_all.58
  281.4 13.7 %all_to_all.64 = bf16[64,8,256]{2,0,1:T(8,128)(2,1)S(1)} all-to-all(bf16[64,8,256]{2,0,1:T(8,128)(2,1)S(1)} %copy.57), channel_id=1, replica_groups=mesh['grp'=4,'seq'=8] {'seq'}, dimensions={1} | all-to-all | bytes 524288 | tf_op jit(solution)/shard_map/all_to_all | solution.py:485
  295.3 1.0 convert_reduce_fusion.4
  296.3 1.4 convolution_convert_fusion.2
  306.2 5.6 %fusion.63 = (bf16[1024,1024]{1,0:T(8,128)(2,1)S(1)}, f32[1024,1024]{1,0:T(8,128)}) fusion(bf16[1024,768]{1,0:T(8,128)(2,1)} %get-tuple-element.72, bf16[768,1024]{1,0:T(8,128)(2,1)} %all-gather.5.cloned.1.call-done), kind=kOutput, calls=%fused_computation.136 | convolution fusion | flops 1611661312 | bytes 9437184 | tf_op jit(solution)/shard_map/dot_general | solution.py:492
  311.8 1.1 fusion.53
  313.8 1.4 collective-permute-start.13
  315.3 1.2 collective-permute-start.14
  316.4 3.8 fusion.64
  320.2 1.2 fusion.54
  322.3 1.4 collective-permute-start.7
  325.1 22.7 %shard_map.291 = (f32[2,64,512]{2,1,0:T(8,128)}, f32[64,128]{1,0:T(8,128)}, f32[2,8,512]{2,1,0:T(8,128)}) custom-call(f32[1,512]{1,0:T(1,128)} %reshape.230.lam_log_ref, f32[1,512]{1,0:T(1,128)} %reshape.231.lam_freq_ref, f32[2,64,512]{2,1,0:T(8,128)} %convert_element_type.235.w_ref, f32[64,1]{1,0:T(8,128)} %copy.53.step_ref, f32[64,16,128]{2,1,0:T(8,128)} %bitcast.93), custom_call_target="tpu_custom_call" | custom-call | tf_op jit(solution)/shard_map/pallas_call | solution.py:337
  348.8 1.4 slice_reduce_fusion
  350.1 1.2 collective-permute-start.8
  351.3 3.6 fusion.19
  355.8 1.4 collective-permute-start.22
  357.2 1.2 collective-permute-start.23
  358.4 8.5 %collective-permute-done.8 = bf16[256,1024]{1,0:T(8,128)(2,1)} collective-permute-done((bf16[256,1024]{1,0:T(8,128)(2,1)}, bf16[256,1024]{1,0:T(8,128)(2,1)}, u32[]{:S(2)}, u32[]{:S(2)}) %collective-permute-start.8) | collective-permute-done | bytes 524320 | tf_op jit(solution)/shard_map/ppermute | solution.py:375
  366.9 3.2 convert_reduce_fusion.3
  370.2 26.5 %all-reduce.1 = f32[8,1344]{1,0:T(8,128)S(1)} all-reduce(f32[8,1344]{1,0:T(8,128)S(1)} %concatenate.19), channel_id=3, replica_groups=mesh['grp'=4,'seq'=8] {'seq'}, use_global_device_ids=true, to_apply=%region_11.12.clone | all-reduce | flops 10752 | bytes 86016
  398.6 1.0 bitcast_convert_fusion.2
  399.6 1.1 copy.61
  401.3 1.2 collective-permute-start.25
  402.5 1.7 collective-permute-start.26
  404.8 1.2 collective-permute-start.19
  406.0 23.5 %all-reduce.7 = (f32[1344]{0:T(1024)S(1)}, f32[64,1024]{1,0:T(8,128)}, f32[64]{0:T(128)}) all-reduce(f32[1344]{0:T(1024)S(1)} %dynamic-slice_reduce_fusion, bf16[64,1024]{1,0:T(8,128)(2,1)} %reduce-scatter.7.cloned.1.call-done, f32[64]{0:T(128)S(1)} %copy-done.12), channel_id=1, replica_groups=mesh['grp'=4,'seq'=8] {'grp'}, use_global_device_ids=true, to_apply=%region_12.13 | all-reduce | flops 66944 | bytes 404480 | tf_op jit(solution)/shard_map/psum | solution.py:532
  432.5 1.6 copy.63
  434.1 3.9 collective-permute-done.20
  438.4 1.4 bitcast_convert_fusion.1
  439.8 1.7 copy.77
  (184 shorter events, 31.0 us)
Async XLA Ops:
  7.2 43.0 %copy-start = (bf16[384,1024]{1,0:T(8,128)(2,1)S(1)}, bf16[384,1024]{1,0:T(8,128)(2,1)}, u32[]{:S(2)}) copy-start(bf16[384,1024]{1,0:T(8,128)(2,1)} %param.21) | copy-start | bytes 2359300
  7.2 3.3 copy-start.13
  7.2 4.5 %copy-start.23 = (s32[1,256]{1,0:T(1,128)S(1)}, s32[1,256]{1,0:T(1,128)}, u32[]{:S(2)}) copy-start(s32[1,256]{1,0:T(1,128)} %param.18) | copy-start | bytes 3076
  7.2 4.5 %copy-start.16 = (bf16[128]{0:T(256)(128)(2,1)S(1)}, bf16[128]{0:T(256)(128)(2,1)}, u32[]{:S(2)}) copy-start(bf16[128]{0:T(256)(128)(2,1)} %param.19) | copy-start | bytes 772
  7.2 4.5 %copy-start.17 = (bf16[128]{0:T(256)(128)(2,1)S(1)}, bf16[128]{0:T(256)(128)(2,1)}, u32[]{:S(2)}) copy-start(bf16[128]{0:T(256)(128)(2,1)} %param.20) | copy-start | bytes 772
  7.2 4.5 %copy-start.14 = (bf16[384]{0:T(512)(128)(2,1)S(1)}, bf16[384]{0:T(512)(128)(2,1)}, u32[]{:S(2)}) copy-start(bf16[384]{0:T(512)(128)(2,1)} %param.22) | copy-start | bytes 2308
  7.3 4.5 %copy-start.18 = (bf16[64]{0:T(256)(128)(2,1)S(1)}, bf16[64]{0:T(256)(128)(2,1)}, u32[]{:S(2)}) copy-start(bf16[64]{0:T(256)(128)(2,1)} %param.24) | copy-start | bytes 388
  7.3 4.5 %copy-start.19 = (bf16[64]{0:T(256)(128)(2,1)S(1)}, bf16[64]{0:T(256)(128)(2,1)}, u32[]{:S(2)}) copy-start(bf16[64]{0:T(256)(128)(2,1)} %param.25) | copy-start | bytes 388
  7.3 4.5 %copy-start.20 = (bf16[64]{0:T(256)(128)(2,1)S(1)}, bf16[64]{0:T(256)(128)(2,1)}, u32[]{:S(2)}) copy-start(bf16[64]{0:T(256)(128)(2,1)} %param.26) | copy-start | bytes 388
  7.3 4.5 %copy-start.15 = (bf16[384]{0:T(512)(128)(2,1)S(1)}, bf16[384]{0:T(512)(128)(2,1)}, u32[]{:S(2)}) copy-start(bf16[384]{0:T(512)(128)(2,1)} %param.30) | copy-start | bytes 2308
  7.3 4.5 %copy-start.21 = (bf16[128]{0:T(256)(128)(2,1)S(1)}, bf16[128]{0:T(256)(128)(2,1)}, u32[]{:S(2)}) copy-start(bf16[128]{0:T(256)(128)(2,1)} %param.32) | copy-start | bytes 772
  7.3 35.4 %copy-start.2 = (bf16[256,1024]{1,0:T(8,128)(2,1)S(1)}, bf16[256,1024]{1,0:T(8,128)(2,1)}, u32[]{:S(2)}) copy-start(bf16[256,1024]{1,0:T(8,128)(2,1)} %param.17) | copy-start | bytes 1572868
  7.3 43.8 %all-gather.7.cloned.1.call-start = ((), (), s32[]{:S(2)}) async-start(), calls=%async_computation.9 | async-start | bytes 1179648 | tf_op jit(solution)/shard_map/all_gather | solution.py:435
  8.0 146.2 %all-gather.9.cloned.1.call-start = ((), (), s32[]{:S(2)}) async-start(), calls=%async_computation.10 | async-start | bytes 1769472 | tf_op jit(solution)/shard_map/all_gather | solution.py:439
  8.1 38.6 %copy-start.3 = (bf16[256,1024]{1,0:T(8,128)(2,1)S(1)}, bf16[256,1024]{1,0:T(8,128)(2,1)}, u32[]{:S(2)}) copy-start(bf16[256,1024]{1,0:T(8,128)(2,1)} %param.33) | copy-start | bytes 1572868
  10.4 169.0 %all-gather.5.cloned.1.call-start = ((), (), s32[]{:S(2)}) async-start(), calls=%async_computation.8 | async-start | bytes 1769472 | tf_op jit(solution)/shard_map/all_gather | solution.py:437
  43.6 135.8 %collective-permute-start = (bf16[256,1024]{1,0:T(8,128)(2,1)S(1)}, bf16[256,1024]{1,0:T(8,128)(2,1)}, u32[]{:S(2)}, u32[]{:S(2)}) collective-permute-start(bf16[256,1024]{1,0:T(8,128)(2,1)S(1)} %fusion.15), channel_id=1, source_target_pairs={{0,8},{8,0},{16,24},{24,16},{1,9},{9,1},{17,25},{25,17},{2,10},{10... | collective-permute-start | bytes 1572872 | tf_op jit(solution)/shard_map/ppermute | solution.py:375
  45.2 134.2 %collective-permute-start.1 = (bf16[256,1024]{1,0:T(8,128)(2,1)S(1)}, bf16[256,1024]{1,0:T(8,128)(2,1)}, u32[]{:S(2)}, u32[]{:S(2)}) collective-permute-start(bf16[256,1024]{1,0:T(8,128)(2,1)S(1)} %fusion.15), channel_id=1, source_target_pairs={{0,16},{8,24},{16,0},{24,8},{1,17},{9,25},{17,1},{25,9},{2,18},{10... | collective-permute-start | bytes 1572872 | tf_op jit(solution)/shard_map/ppermute | solution.py:375
  46.7 97.7 %collective-permute-start.9 = (bf16[256,1024]{1,0:T(8,128)(2,1)S(1)}, bf16[256,1024]{1,0:T(8,128)(2,1)}, u32[]{:S(2)}, u32[]{:S(2)}) collective-permute-start(bf16[256,1024]{1,0:T(8,128)(2,1)S(1)} %copy-done.3), channel_id=1, source_target_pairs={{0,8},{8,0},{16,24},{24,16},{1,9},{9,1},{17,25},{25,17},{2,10},{10... | collective-permute-start | bytes 1572872 | tf_op jit(solution)/shard_map/ppermute | solution.py:375
  47.2 99.6 %collective-permute-start.10 = (bf16[256,1024]{1,0:T(8,128)(2,1)S(1)}, bf16[256,1024]{1,0:T(8,128)(2,1)}, u32[]{:S(2)}, u32[]{:S(2)}) collective-permute-start(bf16[256,1024]{1,0:T(8,128)(2,1)S(1)} %copy-done.3), channel_id=1, source_target_pairs={{0,16},{8,24},{16,0},{24,8},{1,17},{9,25},{17,1},{25,9},{2,18},{10... | collective-permute-start | bytes 1572872 | tf_op jit(solution)/shard_map/ppermute | solution.py:375
  47.7 102.5 %collective-permute-start.11 = (bf16[256,1024]{1,0:T(8,128)(2,1)S(1)}, bf16[256,1024]{1,0:T(8,128)(2,1)S(1)}, u32[]{:S(2)}, u32[]{:S(2)}) collective-permute-start(bf16[256,1024]{1,0:T(8,128)(2,1)S(1)} %copy-done.3), channel_id=1, source_target_pairs={{0,24},{8,16},{16,8},{24,0},{1,25},{9,17},{17,9},{25,1},{2,26},{10... | collective-permute-start | bytes 1572872 | tf_op jit(solution)/shard_map/ppermute | solution.py:375
  50.9 6.4 %copy-start.24 = (bf16[64]{0:T(256)(128)(2,1)S(1)}, bf16[64]{0:T(256)(128)(2,1)}, u32[]{:S(2)}) copy-start(bf16[64]{0:T(256)(128)(2,1)} %param.28) | copy-start | bytes 388
  50.9 7.7 %copy-start.7 = (bf16[2,64,512]{2,1,0:T(8,128)(2,1)S(1)}, bf16[2,64,512]{2,1,0:T(8,128)(2,1)}, u32[]{:S(2)}) copy-start(bf16[2,64,512]{2,1,0:T(8,128)(2,1)} %param.27) | copy-start | bytes 393220
  53.8 45.6 %all-to-all-start = ((bf16[8,64,256]{2,1,0:T(8,128)(2,1)}), bf16[8,64,256]{2,1,0:T(8,128)(2,1)S(1)}, u32[]{:S(2)}, u32[]{:S(2)}) async-start(bf16[8,64,256]{2,1,0:T(8,128)(2,1)} %bitcast.4), calls=%async_computation | async-start | bytes 524288 | tf_op jit(solution)/shard_map/all_to_all | solution.py:465
  119.4 25.0 %all-to-all-start.1 = ((bf16[64,8,256]{2,0,1:T(8,128)(2,1)}), bf16[64,8,256]{2,0,1:T(8,128)(2,1)}, u32[]{:S(2)}, u32[]{:S(2)}) async-start(bf16[64,8,256]{2,0,1:T(8,128)(2,1)} %copy.54), calls=%async_computation.1 | async-start | bytes 524288 | tf_op jit(solution)/shard_map/all_to_all | solution.py:469
  124.4 230.5 %reduce-scatter.9.cloned.1.call-start = ((), (), s32[]{:S(2)}) async-start(), calls=%async_computation.14 | async-start | bytes 884736 | tf_op jit(solution)/shard_map/reduce_scatter | solution.py:496
  144.4 9.4 %collective-permute-start.3 = (bf16[512,256]{1,0:T(8,128)(2,1)}, bf16[512,256]{1,0:T(8,128)(2,1)}, u32[]{:S(2)}, u32[]{:S(2)}) collective-permute-start(bf16[512,256]{1,0:T(8,128)(2,1)} %bitcast.8), channel_id=1, source_target_pairs={{0,8},{8,0},{16,24},{24,16},{1,9},{9,1},{17,25},{25,17},{2,10},{10... | collective-permute-start | bytes 786440 | tf_op jit(solution)/shard_map/ppermute | solution.py:375
  146.8 32.6 %collective-permute-start.2 = (bf16[256,1024]{1,0:T(8,128)(2,1)S(1)}, bf16[256,1024]{1,0:T(8,128)(2,1)}, u32[]{:S(2)}, u32[]{:S(2)}) collective-permute-start(bf16[256,1024]{1,0:T(8,128)(2,1)S(1)} %fusion.15), channel_id=1, source_target_pairs={{0,24},{8,16},{16,8},{24,0},{1,25},{9,17},{17,9},{25,1},{2,26},{10... | collective-permute-start | bytes 1572872 | tf_op jit(solution)/shard_map/ppermute | solution.py:375
  151.0 24.7 %collective-permute-start.4 = (bf16[512,256]{1,0:T(8,128)(2,1)}, bf16[512,256]{1,0:T(8,128)(2,1)S(1)}, u32[]{:S(2)}, u32[]{:S(2)}) collective-permute-start(bf16[512,256]{1,0:T(8,128)(2,1)} %bitcast.8), channel_id=1, source_target_pairs={{0,16},{8,24},{16,0},{24,8},{1,17},{9,25},{17,1},{25,9},{2,18},{10... | collective-permute-start | bytes 786440 | tf_op jit(solution)/shard_map/ppermute | solution.py:375
  153.8 21.9 %collective-permute-start.5 = (bf16[512,256]{1,0:T(8,128)(2,1)}, bf16[512,256]{1,0:T(8,128)(2,1)S(1)}, u32[]{:S(2)}, u32[]{:S(2)}) collective-permute-start(bf16[512,256]{1,0:T(8,128)(2,1)} %bitcast.8), channel_id=1, source_target_pairs={{0,24},{8,16},{16,8},{24,0},{1,25},{9,17},{17,9},{25,1},{2,26},{10... | collective-permute-start | bytes 786440 | tf_op jit(solution)/shard_map/ppermute | solution.py:375
  188.7 1.1 copy-start.4
  192.8 206.8 %reduce-scatter.11.cloned.1.call-start = ((), (), s32[]{:S(2)}) async-start(), calls=%async_computation.15 | async-start | bytes 1769472 | tf_op jit(solution)/shard_map/reduce_scatter | solution.py:496
  197.9 206.3 %reduce-scatter.5.cloned.1.call-start = ((), (), s32[]{:S(2)}) async-start(), calls=%async_computation.11 | async-start | bytes 1769472 | tf_op jit(solution)/shard_map/reduce_scatter | solution.py:496
  205.5 9.2 %collective-permute-start.15 = (bf16[512,256]{1,0:T(8,128)(2,1)S(1)}, bf16[512,256]{1,0:T(8,128)(2,1)S(1)}, u32[]{:S(2)}, u32[]{:S(2)}) collective-permute-start(bf16[512,256]{1,0:T(8,128)(2,1)S(1)} %get-tuple-element.83), channel_id=1, source_target_pairs={{0,8},{8,0},{16,24},{24,16},{1,9},{9,1},{17,25},{25,17},{2,10},{10... | collective-permute-start | bytes 786440 | tf_op jit(solution)/shard_map/ppermute | solution.py:375
  206.1 12.7 %collective-permute-start.16 = (bf16[512,256]{1,0:T(8,128)(2,1)S(1)}, bf16[512,256]{1,0:T(8,128)(2,1)S(1)}, u32[]{:S(2)}, u32[]{:S(2)}) collective-permute-start(bf16[512,256]{1,0:T(8,128)(2,1)S(1)} %get-tuple-element.85), channel_id=1, source_target_pairs={{0,16},{8,24},{16,0},{24,8},{1,17},{9,25},{17,1},{25,9},{2,18},{10... | collective-permute-start | bytes 786440 | tf_op jit(solution)/shard_map/ppermute | solution.py:375
  207.7 12.7 %collective-permute-start.17 = (bf16[512,256]{1,0:T(8,128)(2,1)S(1)}, bf16[512,256]{1,0:T(8,128)(2,1)S(1)}, u32[]{:S(2)}, u32[]{:S(2)}) collective-permute-start(bf16[512,256]{1,0:T(8,128)(2,1)S(1)} %get-tuple-element.84), channel_id=1, source_target_pairs={{0,24},{8,16},{16,8},{24,0},{1,25},{9,17},{17,9},{25,1},{2,26},{10... | collective-permute-start | bytes 786440 | tf_op jit(solution)/shard_map/ppermute | solution.py:375
  221.2 14.2 %all-to-all-start.2 = ((bf16[8,64,256]{2,1,0:T(8,128)(2,1)}), bf16[8,64,256]{2,1,0:T(8,128)(2,1)S(1)}, u32[]{:S(2)}, u32[]{:S(2)}) async-start(bf16[8,64,256]{2,1,0:T(8,128)(2,1)} %bitcast.13), calls=%async_computation.2 | async-start | bytes 524288 | tf_op jit(solution)/shard_map/all_to_all | solution.py:483
  224.7 181.3 %reduce-scatter.7.cloned.1.call-start = ((), (), s32[]{:S(2)}) async-start(), calls=%async_computation.12 | async-start | bytes 1179648 | tf_op jit(solution)/shard_map/reduce_scatter | solution.py:531
  297.8 142.0 %all-reduce.6.cloned.1.call-start = ((), (), s32[]{:S(2)}) async-start(), calls=%async_computation.13 | async-start | bytes 524288 | tf_op jit(solution)/shard_map/psum | solution.py:532
  311.8 4.6 %copy-start.22 = (bf16[1024,768]{0,1:T(8,128)(2,1)S(1)}, bf16[1024,768]{0,1:T(8,128)(2,1)}, u32[]{:S(2)}) copy-start(bf16[1024,768]{0,1:T(8,128)(2,1)} %all-gather.9.cloned.1.call-done) | copy-start | bytes 4718596
  311.8 4.6 %copy-start.25 = (bf16[1024,768]{1,0:T(8,128)(2,1)S(1)}, bf16[1024,768]{1,0:T(8,128)(2,1)}, u32[]{:S(2)}) copy-start(bf16[1024,768]{1,0:T(8,128)(2,1)} %get-tuple-element.74) | copy-start | bytes 4718596
  312.9 37.2 %collective-permute-start.12 = (bf16[256,1024]{1,0:T(8,128)(2,1)}, bf16[256,1024]{1,0:T(8,128)(2,1)}, u32[]{:S(2)}, u32[]{:S(2)}) collective-permute-start(bf16[256,1024]{1,0:T(8,128)(2,1)} %get-tuple-element.77), channel_id=1, source_target_pairs={{0,8},{8,0},{16,24},{24,16},{1,9},{9,1},{17,25},{25,17},{2,10},{10... | collective-permute-start | bytes 1572872 | tf_op jit(solution)/shard_map/ppermute | solution.py:375
  313.8 37.5 %collective-permute-start.13 = (bf16[256,1024]{1,0:T(8,128)(2,1)}, bf16[256,1024]{1,0:T(8,128)(2,1)}, u32[]{:S(2)}, u32[]{:S(2)}) collective-permute-start(bf16[256,1024]{1,0:T(8,128)(2,1)} %get-tuple-element.79), channel_id=1, source_target_pairs={{0,16},{8,24},{16,0},{24,8},{1,17},{9,25},{17,1},{25,9},{2,18},{10... | collective-permute-start | bytes 1572872 | tf_op jit(solution)/shard_map/ppermute | solution.py:375
  315.3 36.1 %collective-permute-start.14 = (bf16[256,1024]{1,0:T(8,128)(2,1)S(1)}, bf16[256,1024]{1,0:T(8,128)(2,1)}, u32[]{:S(2)}, u32[]{:S(2)}) collective-permute-start(bf16[256,1024]{1,0:T(8,128)(2,1)S(1)} %get-tuple-element.78), channel_id=1, source_target_pairs={{0,24},{8,16},{16,8},{24,0},{1,25},{9,17},{17,9},{25,1},{2,26},{10... | collective-permute-start | bytes 1572872 | tf_op jit(solution)/shard_map/ppermute | solution.py:375
  320.2 4.0 copy-start.5
  321.4 35.8 %collective-permute-start.6 = (bf16[256,1024]{1,0:T(8,128)(2,1)}, bf16[256,1024]{1,0:T(8,128)(2,1)S(1)}, u32[]{:S(2)}, u32[]{:S(2)}) collective-permute-start(bf16[256,1024]{1,0:T(8,128)(2,1)} %get-tuple-element.80), channel_id=1, source_target_pairs={{0,8},{8,0},{16,24},{24,16},{1,9},{9,1},{17,25},{25,17},{2,10},{10... | collective-permute-start | bytes 1572872 | tf_op jit(solution)/shard_map/ppermute | solution.py:375
  322.3 36.1 %collective-permute-start.7 = (bf16[256,1024]{1,0:T(8,128)(2,1)}, bf16[256,1024]{1,0:T(8,128)(2,1)S(1)}, u32[]{:S(2)}, u32[]{:S(2)}) collective-permute-start(bf16[256,1024]{1,0:T(8,128)(2,1)} %get-tuple-element.82), channel_id=1, source_target_pairs={{0,16},{8,24},{16,0},{24,8},{1,17},{9,25},{17,1},{25,9},{2,18},{10... | collective-permute-start | bytes 1572872 | tf_op jit(solution)/shard_map/ppermute | solution.py:375
  350.1 16.7 %collective-permute-start.8 = (bf16[256,1024]{1,0:T(8,128)(2,1)}, bf16[256,1024]{1,0:T(8,128)(2,1)}, u32[]{:S(2)}, u32[]{:S(2)}) collective-permute-start(bf16[256,1024]{1,0:T(8,128)(2,1)} %get-tuple-element.81), channel_id=1, source_target_pairs={{0,24},{8,16},{16,8},{24,0},{1,25},{9,17},{17,9},{25,1},{2,26},{10... | collective-permute-start | bytes 1572872 | tf_op jit(solution)/shard_map/ppermute | solution.py:375
  354.9 42.6 %collective-permute-start.21 = (bf16[96,512]{1,0:T(8,128)(2,1)}, bf16[96,512]{1,0:T(8,128)(2,1)S(1)}, u32[]{:S(2)}, u32[]{:S(2)}) collective-permute-start(bf16[96,512]{1,0:T(8,128)(2,1)} %reduce-scatter.9.cloned.1.call-done), channel_id=1, source_target_pairs={{0,8},{8,0},{16,24},{24,16},{1,9},{9,1},{17,25},{25,17},{2,10},{10... | collective-permute-start | bytes 294920 | tf_op jit(solution)/shard_map/ppermute | solution.py:375
  355.8 41.7 %collective-permute-start.22 = (bf16[96,512]{1,0:T(8,128)(2,1)}, bf16[96,512]{1,0:T(8,128)(2,1)S(1)}, u32[]{:S(2)}, u32[]{:S(2)}) collective-permute-start(bf16[96,512]{1,0:T(8,128)(2,1)} %reduce-scatter.9.cloned.1.call-done), channel_id=1, source_target_pairs={{0,16},{8,24},{16,0},{24,8},{1,17},{9,25},{17,1},{25,9},{2,18},{10... | collective-permute-start | bytes 294920 | tf_op jit(solution)/shard_map/ppermute | solution.py:375
  357.2 40.3 %collective-permute-start.23 = (bf16[96,512]{1,0:T(8,128)(2,1)}, bf16[96,512]{1,0:T(8,128)(2,1)}, u32[]{:S(2)}, u32[]{:S(2)}) collective-permute-start(bf16[96,512]{1,0:T(8,128)(2,1)} %reduce-scatter.9.cloned.1.call-done), channel_id=1, source_target_pairs={{0,24},{8,16},{16,8},{24,0},{1,25},{9,17},{17,9},{25,1},{2,26},{10... | collective-permute-start | bytes 294920 | tf_op jit(solution)/shard_map/ppermute | solution.py:375
  366.9 3.2 copy-start.9
  366.9 3.3 copy-start.10
  366.9 3.3 copy-start.11
  366.9 30.6 %copy-start.8 = (bf16[96,512]{1,0:T(8,128)(2,1)S(1)}, bf16[96,512]{1,0:T(8,128)(2,1)}, u32[]{:S(2)}) copy-start(bf16[96,512]{1,0:T(8,128)(2,1)} %reduce-scatter.9.cloned.1.call-done) | copy-start | bytes 294916
  370.1 35.9 %copy-start.12 = (f32[64]{0:T(128)S(1)}, f32[64]{0:T(128)}, u32[]{:S(2)}) copy-start(f32[64]{0:T(128)} %slice_reduce_fusion) | copy-start | bytes 772
  400.7 30.6 %collective-permute-start.24 = (bf16[128,8,96]{0,2,1:T(8,128)(2,1)S(1)}, bf16[128,8,96]{0,2,1:T(8,128)(2,1)S(1)}, u32[]{:S(2)}, u32[]{:S(2)}) collective-permute-start(bf16[128,8,96]{0,2,1:T(8,128)(2,1)S(1)} %bitcast.98), channel_id=1, source_target_pairs={{0,8},{8,0},{16,24},{24,16},{1,9},{9,1},{17,25},{25,17},{2,10},{10... | collective-permute-start | bytes 589832 | tf_op jit(solution)/shard_map/ppermute | solution.py:375
  401.3 30.7 %collective-permute-start.25 = (bf16[128,8,96]{0,2,1:T(8,128)(2,1)S(1)}, bf16[128,8,96]{0,2,1:T(8,128)(2,1)S(1)}, u32[]{:S(2)}, u32[]{:S(2)}) collective-permute-start(bf16[128,8,96]{0,2,1:T(8,128)(2,1)S(1)} %bitcast.99), channel_id=1, source_target_pairs={{0,16},{8,24},{16,0},{24,8},{1,17},{9,25},{17,1},{25,9},{2,18},{10... | collective-permute-start | bytes 589832 | tf_op jit(solution)/shard_map/ppermute | solution.py:375
  402.5 29.6 %collective-permute-start.26 = (bf16[128,8,96]{0,2,1:T(8,128)(2,1)S(1)}, bf16[128,8,96]{0,2,1:T(8,128)(2,1)S(1)}, u32[]{:S(2)}, u32[]{:S(2)}) collective-permute-start(bf16[128,8,96]{0,2,1:T(8,128)(2,1)S(1)} %bitcast.100), channel_id=1, source_target_pairs={{0,24},{8,16},{16,8},{24,0},{1,25},{9,17},{17,9},{25,1},{2,26},{10... | collective-permute-start | bytes 589832 | tf_op jit(solution)/shard_map/ppermute | solution.py:375
  404.2 29.9 %collective-permute-start.18 = (bf16[96,1024]{1,0:T(8,128)(2,1)}, bf16[96,1024]{1,0:T(8,128)(2,1)S(1)}, u32[]{:S(2)}, u32[]{:S(2)}) collective-permute-start(bf16[96,1024]{1,0:T(8,128)(2,1)} %reduce-scatter.5.cloned.1.call-done), channel_id=1, source_target_pairs={{0,8},{8,0},{16,24},{24,16},{1,9},{9,1},{17,25},{25,17},{2,10},{10... | collective-permute-start | bytes 589832 | tf_op jit(solution)/shard_map/ppermute | solution.py:375
  404.8 29.3 %collective-permute-start.19 = (bf16[96,1024]{1,0:T(8,128)(2,1)}, bf16[96,1024]{1,0:T(8,128)(2,1)S(1)}, u32[]{:S(2)}, u32[]{:S(2)}) collective-permute-start(bf16[96,1024]{1,0:T(8,128)(2,1)} %reduce-scatter.5.cloned.1.call-done), channel_id=1, source_target_pairs={{0,16},{8,24},{16,0},{24,8},{1,17},{9,25},{17,1},{25,9},{2,18},{10... | collective-permute-start | bytes 589832 | tf_op jit(solution)/shard_map/ppermute | solution.py:375
  431.3 6.8 %collective-permute-start.20 = (bf16[96,1024]{1,0:T(8,128)(2,1)}, bf16[96,1024]{1,0:T(8,128)(2,1)S(1)}, u32[]{:S(2)}, u32[]{:S(2)}) collective-permute-start(bf16[96,1024]{1,0:T(8,128)(2,1)} %reduce-scatter.5.cloned.1.call-done), channel_id=1, source_target_pairs={{0,24},{8,16},{16,8},{24,0},{1,25},{9,17},{17,9},{25,1},{2,26},{10... | collective-permute-start | bytes 589832 | tf_op jit(solution)/shard_map/ppermute | solution.py:375
  432.5 5.6 %copy-start.6 = (bf16[96,1024]{1,0:T(8,128)(2,1)S(1)}, bf16[96,1024]{1,0:T(8,128)(2,1)}, u32[]{:S(2)}) copy-start(bf16[96,1024]{1,0:T(8,128)(2,1)} %reduce-scatter.5.cloned.1.call-done) | copy-start | bytes 589828
  438.3 3.2 copy-start.1
Sparse Core Ops, SparseCore 0:
  9.7 24.8 all-gather.6
  36.8 29.6 all-gather.8
  68.8 26.1 all-gather.4
  192.9 29.4 reduce-scatter.8
  224.7 33.8 reduce-scatter.10
  260.8 32.6 reduce-scatter.4
  297.9 31.1 reduce-scatter.6
  348.9 48.5 all-reduce.5
where the time goes:
time: 450 us; the launch traced here: 448 us
  Pallas kernels  122 us (27%)
  blocking collectives  113 us (25%)
  waiting for transfers between devices  51.8 us (12%)
  matrix products  50.1 us (11%)
  starting transfers between devices  43 us (10%)
  local copies, waits for them, and re-layouts  34 us (8%)
  between operations  23.1 us (5%)
  other arithmetic  11.6 us (3%)
    unnamed x2, blocking collectives  57 us
    pallas_call x1, Pallas kernels, conv_back(): pl.pallas_call(functools.partial(back_kernel, docs), grid=(channels // RO...  44 us
    ppermute x27, waiting for transfers between devices, swap(): lax.ppermute(x, 'grp', [(i, i ^ k) for i in range(n_grp)])  40.9 us
    pallas_call x1, Pallas kernels, make_toeplitz(): pl.pallas_call(taps_kernel, grid=(channels // ROWS,), in_specs=[pl.BlockS...  37.9 us
    ppermute x27, starting transfers between devices, swap(): lax.ppermute(x, 'grp', [(i, i ^ k) for i in range(n_grp)])  30.6 us
    psum x1, blocking collectives, body(): lax.psum((shard, g_step, g_weights, g_reduce.astype(f32)), 'grp')  23.5 us
    pallas_call x1, Pallas kernels, mode_grads(): pl.pallas_call(mode_grad_kernel, grid=(channels // ROWS,), in_specs=[pl.B...  22.7 us
    all_gather x1, blocking collectives, body(): lax.all_gather(lax.dynamic_slice_in_dim(w_up, me * part, part, 0), 'seq',...  18.8 us
  transfers between devices with their start and end apart: 38, of which 8 were waited for; matrix products, arithmetic and copies ran while one was open for 18% of the time, Pallas kernels for 27%

commit v1 on v0

--- a/solution.py
+++ b/solution.py
@@ -11,6 +11,8 @@
 TILE = 128
 MOST = 2000
 LAGS = 2048
+FINE = 64
+PART = 64
 ROWS = 8
 NT = (((1,), (1,)), ((), ()))
 TN = (((0,), (0,)), ((), ()))
@@ -20,12 +22,25 @@
     return pltpu.CompilerParams(vmem_limit_bytes=mb << 20)
 
 
+def cost(us):
+    return pl.CostEstimate(flops=us * 10**9, bytes_accessed=us * 10**6, transcendentals=0)
+
+
 def lag_blocks(length):
     return min(length // TILE, (MOST + TILE - 2) // TILE + 1)
 
 
 def doc_count(length):
     return length // 1024 + 1
+
+
+def over_channels(step, unroll):
+    def some(i, _):
+        for u in range(unroll):
+            step(i * unroll + u, u)
+        return 0
+
+    lax.fori_loop(0, ROWS // unroll, some, 0)
 
 
 def cmul(a, b):
@@ -78,19 +93,15 @@
     return hi, (x - hi.astype(f32)).astype(bf16)
 
 
-def store_fine(sq_ref, c, qh_ref, ql_ref):
-    width = sq_ref.shape[-1]
-    for t, pair in enumerate(power_tiles(sq_ref, c, 0, TILE // 8)):
-        if t % 2 == 0:
-            held = pair
-            continue
-        for part in range(2):
-            hi, lo = split(jnp.concatenate([held[part], pair[part]], axis=0))
-            qh_ref[8 * t - 8 : 8 * t + 8, part * width : (part + 1) * width] = hi
-            ql_ref[8 * t - 8 : 8 * t + 8, part * width : (part + 1) * width] = lo
-
-
-def taps_kernel(lam_log_ref, lam_freq_ref, w_ref, step_ref, tt_ref, sq_ref, cf_ref, qh_ref, ql_ref, p_ref):
+def coarse_tiles(sq_ref, c):
+    even = power_tiles(sq_ref, c, 7, LAGS // TILE // 8)
+    half = sq_ref[0, 6, pl.ds(c, 1), :], sq_ref[1, 6, pl.ds(c, 1), :]
+    return even + [cmul(t, half) for t in even]
+
+
+def taps_kernel(
+    lam_log_ref, lam_freq_ref, w_ref, step_ref, tt_ref, qh_ref, ql_ref, sq_ref, cf_ref, p_ref
+):
     lam_re, lam_im, delta = mode_rates(lam_log_ref, lam_freq_ref, step_ref)
     one = first_power(lam_re, lam_im, delta)
     store_squares(one, sq_ref)
@@ -103,33 +114,41 @@
     cf_ref[0], cf_ref[1] = cmul((w_ref[0], w_ref[1]), ratio)
     width = sq_ref.shape[-1]
     deep = tt_ref.shape[1]
-    coarse = LAGS // TILE
-
-    def channel(c, _):
-        store_fine(sq_ref, c, qh_ref, ql_ref)
+    coarse = LAGS // FINE
+
+    def channel(c, u):
+        for t, pair in enumerate(power_tiles(sq_ref, c, 0, FINE // 8)):
+            if t % 2 == 0:
+                held = pair
+                continue
+            for part in range(2):
+                hi, lo = split(jnp.concatenate([held[part], pair[part]], axis=0))
+                qh_ref[c, 8 * t - 8 : 8 * t + 8, part * width : (part + 1) * width] = hi
+                ql_ref[c, 8 * t - 8 : 8 * t + 8, part * width : (part + 1) * width] = lo
         coeff = cf_ref[0, pl.ds(c, 1), :], cf_ref[1, pl.ds(c, 1), :]
-        tiles = [cmul(t, coeff) for t in power_tiles(sq_ref, c, 7, coarse // 8)]
+        tiles = [cmul(t, coeff) for t in coarse_tiles(sq_ref, c)]
         for part, sign in ((0, 1.0), (1, -1.0)):
             hi, lo = split(sign * jnp.concatenate([t[part] for t in tiles], axis=0))
-            p_ref[:coarse, part * width : (part + 1) * width] = hi
-            p_ref[coarse:, part * width : (part + 1) * width] = lo
-        both = lax.dot_general(p_ref[...], qh_ref[...], NT, preferred_element_type=f32)
-        low = lax.dot_general(p_ref[:coarse], ql_ref[...], NT, preferred_element_type=f32)
-        taps = both[:coarse] + both[coarse:] + low
+            p_ref[u, :coarse, part * width : (part + 1) * width] = hi
+            p_ref[u, coarse:, part * width : (part + 1) * width] = lo
+        both = lax.dot_general(qh_ref[c], p_ref[u], NT, preferred_element_type=f32)
+        low = lax.dot_general(ql_ref[c], p_ref[u, :coarse], NT, preferred_element_type=f32)
+        taps = (both[:, :coarse] + both[:, coarse:] + low).T
+        taps = jnp.concatenate([taps[: coarse // 2], taps[coarse // 2 :]], axis=1)
         empty = jnp.zeros((TILE, TILE), f32)
         pieces = [empty] + [
-            jnp.broadcast_to(taps[d : d + 1], (TILE, TILE)) if d < coarse else empty for d in range(deep)
+            jnp.broadcast_to(taps[d : d + 1], (TILE, TILE)) if d < LAGS // TILE else empty for d in range(deep)
         ]
         skew = pltpu.roll(jnp.concatenate(pieces, axis=1), 0, 1, stride=1, stride_axis=0)
         for d in range(deep):
             tt_ref[c, d] = skew[:, (d + 1) * TILE : (d + 2) * TILE].astype(bf16)
-        return 0
-
-    lax.fori_loop(0, ROWS, channel, 0)
+
+    over_channels(channel, p_ref.shape[0])
 
 
 def make_toeplitz(lam_log, lam_freq, weights, log_step, deep):
     channels, modes = weights.shape[1:]
+    table = pl.BlockSpec((ROWS, FINE, 2 * modes), lambda i: (i, 0, 0))
     return pl.pallas_call(
         taps_kernel,
         grid=(channels // ROWS,),
@@ -139,16 +158,19 @@
             pl.BlockSpec((2, ROWS, modes), lambda i: (0, i, 0)),
             pl.BlockSpec((ROWS, 1), lambda i: (i, 0)),
         ],
-        out_specs=pl.BlockSpec((ROWS, deep, TILE, TILE), lambda i: (i, 0, 0, 0)),
-        out_shape=jax.ShapeDtypeStruct((channels, deep, TILE, TILE), bf16),
+        out_specs=[pl.BlockSpec((ROWS, deep, TILE, TILE), lambda i: (i, 0, 0, 0)), table, table],
+        out_shape=[
+            jax.ShapeDtypeStruct((channels, deep, TILE, TILE), bf16),
+            jax.ShapeDtypeStruct((channels, FINE, 2 * modes), bf16),
+            jax.ShapeDtypeStruct((channels, FINE, 2 * modes), bf16),
+        ],
         scratch_shapes=[
             pltpu.VMEM((2, 11, ROWS, modes), f32),
             pltpu.VMEM((2, ROWS, modes), f32),
-            pltpu.VMEM((TILE, 2 * modes), bf16),
-            pltpu.VMEM((TILE, 2 * modes), bf16),
-            pltpu.VMEM((2 * LAGS // TILE, 2 * modes), bf16),
+            pltpu.VMEM((4, 2 * LAGS // FINE, 2 * modes), bf16),
         ],
         compiler_params=params(),
+        cost_estimate=cost(25),
     )(lam_log[None], lam_freq[None], weights, log_step[:, None])
 
 
@@ -183,7 +205,7 @@
     lax.fori_loop(0, ROWS // xs_ref.shape[0], pair, 0)
 
 
-def conv(seg, x, tt, unroll=2):
+def conv(seg, x, tt, unroll=4):
     channels, blocks, _ = x.shape
     deep = tt.shape[1]
     docs = doc_count(blocks * TILE)
@@ -202,42 +224,35 @@
             pltpu.VMEM((unroll, docs * blocks, deep * TILE), bf16),
         ],
         compiler_params=params(),
+        cost_estimate=cost(17),
     )(seg, x, tt)
 
 
-def back_kernel(docs, seg_ref, flip_ref, x_ref, g_ref, tt_ref, gx_ref, dt_ref, gs_ref, gw_ref, xst_ref):
-    blocks, deep = x_ref.shape[1], tt_ref.shape[1]
+def back_kernel(docs, seg_ref, flip_ref, g_ref, tt_ref, gx_ref, gs_ref, gw_ref, gr_ref):
+    blocks, deep = g_ref.shape[1], tt_ref.shape[1]
     lead = deep - 1
-    seg = seg_ref[...]
+    flip = flip_ref[...]
+    seg = jnp.dot(seg_ref[...].astype(bf16), flip, preferred_element_type=f32)
+    flat = g_ref[...].reshape(ROWS * blocks, TILE)
+    gr_ref[...] = jnp.dot(flat, flip, preferred_element_type=f32).reshape(gr_ref.shape)
     for u in range(gs_ref.shape[0]):
         for k in range(docs):
             gs_ref[u, k, blocks:, :] = jnp.zeros((lead, TILE), f32)
 
     def one(c, u):
-        g = g_ref[c].astype(f32)
-        x = x_ref[c].astype(f32)
+        g = gr_ref[c]
         for k in range(docs):
             gs_ref[u, k, :blocks, :] = jnp.where(seg == k, g, 0.0)
-            xst_ref[u, k * blocks : (k + 1) * blocks, :] = jnp.where(seg == k, x, 0.0).astype(bf16)
         for k in range(docs):
             for d in range(deep):
                 gw_ref[u, k * blocks : (k + 1) * blocks, d * TILE : (d + 1) * TILE] = gs_ref[
                     u, k, d : d + blocks, :
                 ].astype(bf16)
-        gx = jnp.zeros((docs * blocks, TILE), f32)
-        for d in range(deep):
-            gx += lax.dot_general(
-                gw_ref[u, :, d * TILE : (d + 1) * TILE], tt_ref[c, d], NT, preferred_element_type=f32
-            )
+        gx = jnp.dot(gw_ref[u], tt_ref[c].reshape(deep * TILE, TILE), preferred_element_type=f32)
         out = jnp.zeros((blocks, TILE), f32)
         for k in range(docs):
             out = jnp.where(seg == k, gx[k * blocks : (k + 1) * blocks], out)
-        gx_ref[c] = out.astype(bf16)
-        xr = jnp.dot(xst_ref[u], flip_ref[...], preferred_element_type=f32).astype(bf16)
-        wide = lax.dot_general(xr, gw_ref[u], TN, preferred_element_type=f32)
-        wide = jnp.concatenate([wide, jnp.zeros((TILE, TILE), f32)], axis=1)
-        flat = pltpu.roll(wide, wide.shape[1] - (TILE - 1), 1, stride=1, stride_axis=0)
-        dt_ref[pl.ds(c, 1), :] = jnp.sum(flat[:, : LAGS], axis=0, keepdims=True)
+        gr_ref[c] = out
 
     def pair(i, _):
         for u in range(gs_ref.shape[0]):
@@ -245,10 +260,12 @@
         return 0
 
     lax.fori_loop(0, ROWS // gs_ref.shape[0], pair, 0)
-
-
-def conv_back(seg, x, g, tt, unroll=2):
-    channels, blocks, _ = x.shape
+    flat = gr_ref[...].astype(bf16).reshape(ROWS * blocks, TILE)
+    gx_ref[...] = jnp.dot(flat, flip, preferred_element_type=f32).astype(bf16).reshape(gx_ref.shape)
+
+
+def conv_back(seg, g, tt, unroll=4):
+    channels, blocks, _ = g.shape
     deep = tt.shape[1]
     docs = doc_count(blocks * TILE)
     flip = jnp.eye(TILE, dtype=bf16)[::-1]
@@ -260,51 +277,124 @@
             pl.BlockSpec((blocks, TILE), lambda i: (0, 0)),
             pl.BlockSpec((TILE, TILE), lambda i: (0, 0)),
             rows,
-            rows,
             pl.BlockSpec((ROWS, deep, TILE, TILE), lambda i: (i, 0, 0, 0)),
         ],
-        out_specs=[rows, pl.BlockSpec((ROWS, LAGS), lambda i: (i, 0))],
-        out_shape=[jax.ShapeDtypeStruct(x.shape, bf16), jax.ShapeDtypeStruct((channels, LAGS), f32)],
+        out_specs=rows,
+        out_shape=jax.ShapeDtypeStruct(g.shape, bf16),
         scratch_shapes=[
             pltpu.VMEM((unroll, docs, blocks + deep - 1, TILE), f32),
             pltpu.VMEM((unroll, docs * blocks, deep * TILE), bf16),
-            pltpu.VMEM((unroll, docs * blocks, TILE), bf16),
+            pltpu.VMEM((ROWS, blocks, TILE), f32),
         ],
         compiler_params=params(),
-    )(seg, flip, x, g, tt)
+        cost_estimate=cost(15),
+    )(seg, flip, g, tt)
+
+
+def taps_grad_kernel(docs, seg_ref, flip_ref, x_ref, g_ref, dt_ref, gs_ref, gw_ref, xst_ref):
+    blocks = x_ref.shape[1]
+    deep = gw_ref.shape[2] // TILE
+    lead = deep - 1
+    cuts = TILE // PART
+    seg = seg_ref[...]
+    lane = lax.broadcasted_iota(jnp.int32, (blocks, TILE), 1)
+    for u in range(gs_ref.shape[0]):
+        for k in range(docs * cuts):
+            gs_ref[u, k, blocks:, :] = jnp.zeros((lead, TILE), f32)
+
+    def one(c, u):
+        g = g_ref[c].astype(f32)
+        x = x_ref[c].astype(f32)
+        for k in range(docs):
+            own = jnp.where(seg == k, g, 0.0)
+            gs_ref[u, k * cuts, :blocks, :] = own
+            after = jnp.concatenate([own[1:], jnp.zeros((1, TILE), f32)], axis=0)
+            for p in range(1, cuts):
+                gs_ref[u, k * cuts + p, :blocks, :] = pltpu.roll(
+                    jnp.where(lane < p * PART, after, own), TILE - p * PART, 1
+                )
+            mine = jnp.where(seg == k, x, 0.0).astype(bf16)
+            mine = jnp.dot(mine, flip_ref[...], preferred_element_type=f32).astype(bf16)
+            for p in range(cuts):
+                at = (k * cuts + p) * blocks
+                xst_ref[u, at : at + blocks, :] = mine[:, p * PART : (p + 1) * PART]
+        for k in range(docs * cuts):
+            for d in range(deep):
+                gw_ref[u, k * blocks : (k + 1) * blocks, d * TILE : (d + 1) * TILE] = gs_ref[
+                    u, k, d : d + blocks, :
+                ].astype(bf16)
+        wide = lax.dot_general(xst_ref[u], gw_ref[u], TN, preferred_element_type=f32)
+        wide = jnp.concatenate([wide, jnp.zeros((PART, TILE), f32)], axis=1)
+        flat = pltpu.roll(wide, wide.shape[1] - (PART - 1), 1, stride=1, stride_axis=0)
+        dt_ref[pl.ds(c, 1), :] = jnp.sum(flat[:, :LAGS], axis=0, keepdims=True)
+
+    def pair(i, _):
+        for u in range(gs_ref.shape[0]):
+            one(i * gs_ref.shape[0] + u, u)
+        return 0
+
+    lax.fori_loop(0, ROWS // gs_ref.shape[0], pair, 0)
+
+
+def taps_grad(seg, x, g, unroll=4):
+    channels, blocks, _ = x.shape
+    deep = lag_blocks(blocks * TILE)
+    docs = doc_count(blocks * TILE)
+    cuts = TILE // PART
+    place = jnp.arange(TILE)
+    flip = (place[:, None] == (place // PART * PART + PART - 1 - place % PART)[None, :]).astype(bf16)
+    rows = pl.BlockSpec((ROWS, blocks, TILE), lambda i: (i, 0, 0))
+    return pl.pallas_call(
+        functools.partial(taps_grad_kernel, docs),
+        grid=(channels // ROWS,),
+        in_specs=[
+            pl.BlockSpec((blocks, TILE), lambda i: (0, 0)),
+            pl.BlockSpec((TILE, TILE), lambda i: (0, 0)),
+            rows,
+            rows,
+        ],
+        out_specs=pl.BlockSpec((ROWS, LAGS), lambda i: (i, 0)),
+        out_shape=jax.ShapeDtypeStruct((channels, LAGS), f32),
+        scratch_shapes=[
+            pltpu.VMEM((unroll, docs * cuts, blocks + deep - 1, TILE), f32),
+            pltpu.VMEM((unroll, docs * cuts * blocks, deep * TILE), bf16),
+            pltpu.VMEM((unroll, docs * cuts * blocks, PART), bf16),
+        ],
+        compiler_params=params(),
+        cost_estimate=cost(20),
+    )(seg, flip, x, g)
 
 
 def mode_grad_kernel(
-    lam_log_ref, lam_freq_ref, w_ref, step_ref, dt_ref, gw_ref, gstep_ref, glam_ref, sq_ref, qh_ref, ql_ref, l_ref, s_ref
+    lam_log_ref, lam_freq_ref, w_ref, step_ref, dt_ref, qh_ref, ql_ref, gw_ref, gstep_ref, glam_ref, sq_ref, s_ref
 ):
     lam_re, lam_im, delta = mode_rates(lam_log_ref, lam_freq_ref, step_ref)
     one = first_power(lam_re, lam_im, delta)
     store_squares(one, sq_ref)
     width = sq_ref.shape[-1]
-    coarse = LAGS // TILE
-
-    def channel(c, _):
-        store_fine(sq_ref, c, qh_ref, ql_ref)
+    coarse = LAGS // FINE
+
+    def channel(c, u):
         dt = dt_ref[c]
-        lane = lax.broadcasted_iota(jnp.int32, (coarse, TILE), 1).astype(f32)
+        dt = jnp.concatenate([dt[:, :FINE], dt[:, FINE:]], axis=0)
+        lane = lax.broadcasted_iota(jnp.int32, (coarse, FINE), 1).astype(f32)
         hi, lo = split(jnp.concatenate([dt, dt * lane], axis=0))
-        l_ref[: 2 * coarse] = hi
-        l_ref[2 * coarse :] = lo
-        both = jnp.dot(l_ref[...], qh_ref[...], preferred_element_type=f32)
-        low = jnp.dot(l_ref[: 2 * coarse], ql_ref[...], preferred_element_type=f32)
+        both = jnp.dot(jnp.concatenate([hi, lo], axis=0), qh_ref[c], preferred_element_type=f32)
+        low = jnp.dot(hi, ql_ref[c], preferred_element_type=f32)
         v = both[: 2 * coarse] + both[2 * coarse :] + low
-        tiles = power_tiles(sq_ref, c, 7, coarse // 8)
+        tiles = coarse_tiles(sq_ref, c)
         power = tuple(jnp.concatenate([t[part] for t in tiles], axis=0) for part in range(2))
         v0 = v[:coarse, :width], v[:coarse, width:]
-        row = lax.broadcasted_iota(jnp.int32, (coarse, width), 0).astype(f32) * float(TILE)
-        v1 = tuple(row * v0[part] + v[coarse:, part * width : (part + 1) * width] for part in range(2))
+        row = lax.broadcasted_iota(jnp.int32, (coarse, width), 0)
+        far = (row % (coarse // 2)) * (2 * FINE) + (row // (coarse // 2)) * FINE
+        far = far.astype(f32)
+        v1 = tuple(far * v0[part] + v[coarse:, part * width : (part + 1) * width] for part in range(2))
         for n, pair in enumerate((v0, v1)):
             prod = cmul(power, pair)
             for part in range(2):
                 s_ref[2 * n + part, pl.ds(c, 1), :] = jnp.sum(prod[part], axis=0, keepdims=True)
-        return 0
-
-    lax.fori_loop(0, ROWS, channel, 0)
+
+    over_channels(channel, 4)
     modulus = lam_re * lam_re + lam_im * lam_im
     inv = lam_re / modulus, -lam_im / modulus
     shift = one[0] - 1.0, one[1]
@@ -331,9 +421,10 @@
     glam_ref[1] -= big[1]
 
 
-def mode_grads(lam_log, lam_freq, weights, log_step, dt):
+def mode_grads(lam_log, lam_freq, weights, log_step, dt, fine_high, fine_low):
     channels, modes = weights.shape[1:]
-    coarse = LAGS // TILE
+    rows = LAGS // TILE
+    table = pl.BlockSpec((ROWS, FINE, 2 * modes), lambda i: (i, 0, 0))
     gw, gstep, glam = pl.pallas_call(
         mode_grad_kernel,
         grid=(channels // ROWS,),
@@ -342,7 +433,9 @@
             pl.BlockSpec((1, modes), lambda i: (0, 0)),
             pl.BlockSpec((2, ROWS, modes), lambda i: (0, i, 0)),
             pl.BlockSpec((ROWS, 1), lambda i: (i, 0)),
-            pl.BlockSpec((ROWS, coarse, TILE), lambda i: (i, 0, 0)),
+            pl.BlockSpec((ROWS, rows, TILE), lambda i: (i, 0, 0)),
+            table,
+            table,
         ],
         out_specs=[
             pl.BlockSpec((2, ROWS, modes), lambda i: (0, i, 0)),
@@ -356,13 +449,11 @@
         ],
         scratch_shapes=[
             pltpu.VMEM((2, 11, ROWS, modes), f32),
-            pltpu.VMEM((TILE, 2 * modes), bf16),
-            pltpu.VMEM((TILE, 2 * modes), bf16),
-            pltpu.VMEM((4 * coarse, TILE), bf16),
             pltpu.VMEM((4, ROWS, modes), f32),
         ],
         compiler_params=params(),
-    )(lam_log[None], lam_freq[None], weights, log_step[:, None], dt.reshape(channels, coarse, TILE))
+        cost_estimate=cost(12),
+    )(lam_log[None], lam_freq[None], weights, log_step[:, None], dt.reshape(channels, rows, TILE), fine_high, fine_low)
     return gw, gstep[:, 0], jnp.sum(glam, axis=1)
 
 
@@ -384,6 +475,16 @@
     for k in range(1, n_grp):
         total = total + swap(pieces[k].astype(bf16), k, n_grp).astype(f32)
     return total
+
+
+def tree_sum(terms):
+    while len(terms) > 1:
+        terms = [terms[i] + terms[i + 1] for i in range(0, len(terms), 2)]
+    return terms[0]
+
+
+def sum_grp(x, n_grp):
+    return tree_sum([y.astype(f32) for y in gather_grp(x.astype(bf16), n_grp)])
 
 
 def place_grp(x, n_grp, me, axis):
@@ -421,7 +522,9 @@
     reduced_width = w_reduce.shape[0] * n_seq
 
     small = (ln_gain, ln_bias, b_value, b_reduce, lam_log, lam_freq, b_up, b_out, segments[0].astype(bf16))
-    packed = lax.all_gather(jnp.concatenate(small), "seq", axis=0)
+    packed = jnp.concatenate(small)
+    packed = jnp.pad(packed, (0, -packed.shape[0] % 2048)).reshape(-1, 128)
+    packed = lax.all_gather(packed, "seq", axis=0, tiled=True).reshape(n_seq, -1)
     spots, fulls = 0, []
     for array in small:
         fulls.append(packed[:, spots : spots + array.shape[0]])
@@ -433,8 +536,9 @@
     up_bias = lax.dynamic_slice_in_dim(up_bias, me * part, part, 1).reshape(-1).astype(f32)
 
     reduce_full = lax.all_gather(w_reduce, "seq", axis=0, tiled=True)
-    up_part = lax.all_gather(lax.dynamic_slice_in_dim(w_up, me * part, part, 0), "seq", axis=0, tiled=True)
-    value_part = lax.all_gather(lax.dynamic_slice_in_dim(w_value, me * part, part, 0), "seq", axis=0, tiled=True)
+    pieces = [lax.dynamic_slice_in_dim(w, me * part, part, 0) for w in (w_value, w_up)]
+    both_part = lax.all_gather(jnp.concatenate(pieces, axis=1), "seq", axis=0, tiled=True)
+    value_part, up_part = both_part[:, :wide], both_part[:, wide:]
     out_cols = lax.dynamic_index_in_dim(w_out.reshape(-1, n_seq, n_grp, part), me, 2, keepdims=False)
     out_part = lax.all_gather(out_cols.reshape(-1, quarter), "seq", axis=0, tiled=True)
 
@@ -446,7 +550,7 @@
     )
     length = tokens * n_seq
     blocks = length // TILE
-    toeplitz = make_toeplitz(*modes, lag_blocks(length))
+    toeplitz, fine_high, fine_low = make_toeplitz(*modes, lag_blocks(length))
 
     x_wide = layer_input.astype(f32)
     center = x_wide - jnp.mean(x_wide, axis=1, keepdims=True)
@@ -481,9 +585,15 @@
     g_mixed = lax.dot_general(up_part, g_pre_up, (((0,), (1,)), ((), ())), preferred_element_type=f32)
     g_mixed = sum_scatter_grp([g_mixed[:, k * tokens : (k + 1) * tokens] for k in range(n_grp)], n_grp)
     g_channel = lax.all_to_all(g_mixed.astype(bf16), "seq", split_axis=0, concat_axis=1, tiled=True)
-    g_signal, g_taps = conv_back(seg, signal, g_channel.reshape(-1, blocks, TILE), toeplitz)
+    g_channel = g_channel.reshape(-1, blocks, TILE)
+    g_signal = conv_back(seg, g_channel, toeplitz)
     g_reduced = lax.all_to_all(g_signal.reshape(-1, length), "seq", split_axis=1, concat_axis=0, tiled=True)
-    g_weights, g_step, g_lam = mode_grads(*modes, g_taps)
+    g_taps = taps_grad(seg, signal, g_channel)
+    g_weights, g_step, g_lam = mode_grads(*modes, g_taps, fine_high, fine_low)
+    channels, states = g_weights.shape[1:]
+    own = jnp.concatenate([g_weights.reshape(-1), jnp.pad(g_step, (0, -channels % states))])
+    own = sum_grp(own.reshape(-1, states), n_grp)
+    g_weights, g_step = own[: 2 * channels].reshape(g_weights.shape), own[2 * channels :].reshape(-1)[:channels]
 
     added = lax.dot_general(gated, out_part, contract_last, preferred_element_type=f32)
     added = sum_scatter_grp([added[k * tokens : (k + 1) * tokens] for k in range(n_grp)], n_grp)
@@ -496,11 +606,12 @@
         return lax.psum_scatter(x.astype(bf16), "seq", scatter_dimension=0, tiled=True)
 
     g_out = over_seq(lax.dot_general(cot_all, gated, contract_first, preferred_element_type=f32))
-    g_up = over_seq(lax.dot_general(g_pre_up, mixed_all, (((0,), (1,)), ((), ())), preferred_element_type=f32))
-    g_value = over_seq(lax.dot_general(g_pre_value, normed_all, contract_first, preferred_element_type=f32))
+    g_up = lax.dot_general(g_pre_up, mixed_all, (((0,), (1,)), ((), ())), preferred_element_type=f32)
+    g_value = lax.dot_general(g_pre_value, normed_all, contract_first, preferred_element_type=f32)
+    g_both = over_seq(jnp.concatenate([g_value.astype(bf16), g_up.astype(bf16)], axis=1))
     g_out = place_grp(g_out.reshape(-1, n_seq, part), n_grp, me, 2).reshape(w_out.shape).astype(f32)
-    g_up = place_grp(g_up, n_grp, me, 0).reshape(w_up.shape).astype(f32)
-    g_value = place_grp(g_value, n_grp, me, 0).reshape(w_value.shape).astype(f32)
+    g_both = place_grp(g_both, n_grp, me, 0).reshape(-1, g_both.shape[1]).astype(f32)
+    g_value, g_up = g_both[:, :wide], g_both[:, wide:]
 
     g_pre_reduce = reduce_pull(g_reduced.astype(f32))[0].astype(bf16)
     g_reduce = jnp.dot(g_pre_reduce, normed, preferred_element_type=f32)
@@ -527,11 +638,11 @@
         spread(jnp.sum(g_pre_up.astype(f32), axis=0)),
         jnp.sum(out_cotangent.astype(f32), axis=0).reshape(n_seq, -1),
     )
-    shard = lax.psum_scatter(jnp.concatenate(vectors, axis=1), "seq", scatter_dimension=0, tiled=False)
-    g_reduce = lax.psum_scatter(g_reduce.astype(bf16), "seq", scatter_dimension=0, tiled=True)
-    shard, g_step, g_weights, g_reduce = lax.psum(
-        (shard, g_step, g_weights, g_reduce.astype(f32)), "grp"
-    )
+    flat = jnp.concatenate(vectors, axis=1)
+    flat = jnp.pad(flat, ((0, 0), (0, -flat.shape[1] % wide))).reshape(n_seq, -1, wide)
+    own = jnp.concatenate([g_reduce.reshape(n_seq, -1, wide).astype(bf16), flat.astype(bf16)], axis=1)
+    own = sum_grp(lax.psum_scatter(own, "seq", scatter_dimension=0, tiled=False), n_grp)
+    g_reduce, shard = own[: w_reduce.shape[0]], own[w_reduce.shape[0] :].reshape(-1)
     sums, spots = [], 0
     for array in vectors:
         sums.append(shard[spots : spots + array.shape[1]])

time: 450 us -> 377 us (0.84)
  blocking collectives: 113 us -> 15.7 us
  waiting for transfers between devices: 51.8 us -> 82.8 us
  Pallas kernels: 122 us -> 108 us
  starting transfers between devices: 43 us -> 51 us
  matrix products: 50.1 us -> 43.6 us
  other arithmetic: 11.6 us -> 17.8 us
    unnamed x2 -> x0, blocking collectives: 57 us -> none
    pallas_call x0 -> x1, Pallas kernels: none -> 28.7 us  [taps_grad(): pl.pallas_call(functools.partial(taps_grad_kernel, docs), grid=(channels...]
    pallas_call x1, Pallas kernels: 44 us -> 17.1 us  [conv_back(): pl.pallas_call(functools.partial(back_kernel, docs), grid=(channels // RO...]
    psum x1 -> x0, blocking collectives: 23.5 us -> none  [body(): lax.psum((shard, g_step, g_weights, g_reduce.astype(f32)), 'grp')]
    all_to_all x1, waiting for transfers between devices: 0.01 us -> 15.6 us  [body(): lax.all_to_all(reduced.astype(bf16), 'seq', split_axis=0, concat_axis=1,...]
    ppermute x27 -> x30, waiting for transfers between devices: 40.9 us -> 54.9 us  [swap(): lax.ppermute(x, 'grp', [(i, i ^ k) for i in range(n_grp)])]
    all_to_all x1 -> x0, blocking collectives: 13.7 us -> none  [body(): lax.all_to_all(g_signal.reshape(-1, length), 'seq', split_axis=1, concat_...]
    pallas_call x1, Pallas kernels: 37.9 us -> 30.2 us  [make_toeplitz(): pl.pallas_call(taps_kernel, grid=(channels // ROWS,), in_specs=[pl.BlockS...]
  transfers between devices with their start and end apart: 38 -> 40, of which waited for: 8 -> 20; matrix products, arithmetic and copies ran while one was open for 18% -> 21% of each run, Pallas kernels for 27% -> 29%
where the time goes in v1:
time: 377 us; the launch traced here: 375 us
  Pallas kernels  108 us (29%)
  waiting for transfers between devices  82.8 us (22%)
  starting transfers between devices  51 us (14%)
  matrix products  43.6 us (12%)
  local copies, waits for them, and re-layouts  34.2 us (9%)
  between operations  22.7 us (6%)
  other arithmetic  17.8 us (5%)
  blocking collectives  15.7 us (4%)
    ppermute x30, waiting for transfers between devices, swap(): lax.ppermute(x, 'grp', [(i, i ^ k) for i in range(n_grp)])  54.9 us
    ppermute x30, starting transfers between devices, swap(): lax.ppermute(x, 'grp', [(i, i ^ k) for i in range(n_grp)])  35.4 us
    pallas_call x1, Pallas kernels, make_toeplitz(): pl.pallas_call(taps_kernel, grid=(channels // ROWS,), in_specs=[pl.BlockS...  30.2 us
    pallas_call x1, Pallas kernels, taps_grad(): pl.pallas_call(functools.partial(taps_grad_kernel, docs), grid=(channels...  28.7 us
    pallas_call x1, Pallas kernels, conv_back(): pl.pallas_call(functools.partial(back_kernel, docs), grid=(channels // RO...  17.1 us
    pallas_call x1, Pallas kernels, conv(): pl.pallas_call(functools.partial(conv_kernel, docs), grid=(channels // RO...  16.3 us
    all_gather x1, blocking collectives, body(): lax.all_gather(packed, 'seq', axis=0, tiled=True).reshape(n_seq, -1)  15.7 us
    all_to_all x1, waiting for transfers between devices, body(): lax.all_to_all(reduced.astype(bf16), 'seq', split_axis=0, concat_axis=1,...  15.6 us
  transfers between devices with their start and end apart: 40, of which 20 were waited for; matrix products, arithmetic and copies ran while one was open for 21% of the time, Pallas kernels for 29%

profile of v1, /device:TPU:0, one launch (start us, length us, event | category | flops | bytes accessed | tf_op | source)
XLA Modules:
  0.0 375.5 jit_solution(18264712443824429697)
XLA Ops:
  8.1 1.6 copy.57
  10.7 15.7 %all_gather.12 = bf16[128,128]{1,0:T(8,128)(2,1)S(1)} all-gather(bf16[16,128]{1,0:T(8,128)(2,1)S(1)} %pad_bitcast_fusion), channel_id=1, replica_groups=mesh['grp'=4,'seq'=8] {'seq'}, dimensions={0}, use_global_device_ids=true | all-gather | bytes 36864 | tf_op jit(solution)/shard_map/all_gather | solution.py:527
  27.3 1.6 collective-permute-start
  28.8 1.5 collective-permute-start.1
  31.4 2.4 collective-permute-start.11
  39.8 30.2 %shard_map.288 = (bf16[64,16,128,128]{3,2,1,0:T(8,128)(2,1)}, bf16[64,64,1024]{2,1,0:T(8,128)(2,1)}, bf16[64,64,1024]{2,1,0:T(8,128)(2,1)}) custom-call(f32[1,512]{1,0:T(1,128)} %reshape.285.lam_log_ref, f32[1,512]{1,0:T(1,128)} %reshape.286.lam_freq_ref, f32[2,64,512]{2,1,0:T(8,128)} %convert_element_type.270.w_ref, f32[64,1]{1,0:T(8,128)} %copy.55.step_ref), custom_call_target="tpu_custom_call" | custom-call | flops 24999999488 | bytes 25000000 | tf_op jit(solution)/shard_map/pallas_call | solution.py:152
  70.2 2.6 multiply_convert_fusion.2
  73.6 4.6 %all-to-all-start = ((bf16[8,64,256]{2,1,0:T(8,128)(2,1)}), bf16[8,64,256]{2,1,0:T(8,128)(2,1)S(1)}, u32[]{:S(2)}, u32[]{:S(2)}) async-start(bf16[8,64,256]{2,1,0:T(8,128)(2,1)} %bitcast.4), calls=%async_computation | async-start | bytes 524288 | tf_op jit(solution)/shard_map/all_to_all | solution.py:569
  79.5 15.6 %all-to-all-done = bf16[8,64,256]{2,1,0:T(8,128)(2,1)S(1)} async-done(((bf16[8,64,256]{2,1,0:T(8,128)(2,1)}), bf16[8,64,256]{2,1,0:T(8,128)(2,1)S(1)}, u32[]{:S(2)}, u32[]{:S(2)}) %all-to-all-start) | async-done | bytes 262176 | tf_op jit(solution)/shard_map/all_to_all | solution.py:569
  96.1 16.3 %shard_map.289 = bf16[64,16,128]{2,1,0:T(8,128)(2,1)} custom-call(s32[16,128]{1,0:T(8,128)} %reshape.283.seg_ref, bf16[64,16,128]{2,1,0:T(8,128)(2,1)} %reshape.262.x_ref, bf16[64,16,128,128]{3,2,1,0:T(8,128)(2,1)} %get-tuple-element.22.tt_ref), custom_call_target="tpu_custom_call" | custom-call | flops 16999999488 | bytes 17000000 | tf_op jit(solution)/shard_map/pallas_call | solution.py:212
  114.2 3.4 all-to-all-start.1
  119.6 7.6 %all-to-all-done.1 = bf16[64,8,256]{2,0,1:T(8,128)(2,1)S(1)} async-done(((bf16[64,8,256]{2,0,1:T(8,128)(2,1)}), bf16[64,8,256]{2,0,1:T(8,128)(2,1)S(1)}, u32[]{:S(2)}, u32[]{:S(2)}) %all-to-all-start.1) | async-done | bytes 262176 | tf_op jit(solution)/shard_map/all_to_all | solution.py:573
  128.2 1.9 constant_dynamic-update-slice_fusion.2
  130.1 1.4 collective-permute-start.2
  133.2 1.1 collective-permute-start.4
  134.3 2.2 collective-permute-done.3
  137.9 5.6 %fusion.80 = f32[1024,768]{1,0:T(8,128)} fusion(bf16[1024,1024]{1,0:T(8,128)(2,1)} %constant_dynamic-update-slice_fusion, bf16[1024,768]{0,1:T(8,128)(2,1)} %all-gather.8.cloned.1.call-done), kind=kOutput, calls=%fused_computation.160 | convolution fusion | flops 1610612736 | bytes 6815744 | tf_op jit(solution)/shard_map/dot_general | solution.py:578
  143.5 13.2 %collective-permute-done.4 = bf16[512,256]{1,0:T(8,128)(2,1)S(1)} collective-permute-done((bf16[512,256]{1,0:T(8,128)(2,1)S(1)}, bf16[512,256]{1,0:T(8,128)(2,1)S(1)}, u32[]{:S(2)}, u32[]{:S(2)}) %collective-permute-start.4) | collective-permute-done | bytes 262176 | tf_op jit(solution)/shard_map/ppermute | solution.py:466
  156.8 2.3 fusion.35
  159.8 7.7 %convert_reduce_fusion.1 = (bf16[768]{0:T(1024)(128)(2,1)S(1)}, bf16[1024,768]{1,0:T(8,128)(2,1)}, bf16[1024,768]{1,0:T(8,128)(2,1)S(1)}, bf16[768]{0:T(1024)(128)(2,1)S(1)}, bf16[1024,768]{1,0:T(8,128)(2,1)S(1)}) fusion(f32[768]{0:T(1024)S(1)} %reshape.281, f32[1024,768]{1,0:T(8,128)S(1)} %copy-done.38, f32[1024,768]{1,0:T(8,128)S(1)} %fusion.35, ...), kind=kOutput, calls=%fused_computation.10 | convolution fusion | flops 1644165632 | bytes 14691328 | tf_op jit(solution)/shard_map/dot_general | solution.py:576
  169.8 1.7 collective-permute-start.16
  171.6 1.4 collective-permute-start.17
  173.0 3.2 convolution_convert_fusion
  176.1 2.8 collective-permute-done.15
  178.9 3.1 collective-permute-done.16
  182.0 1.2 collective-permute-done.17
  183.2 1.8 fusion.46
  184.9 3.8 %all-to-all-start.2 = ((bf16[8,64,256]{2,1,0:T(8,128)(2,1)}), bf16[8,64,256]{2,1,0:T(8,128)(2,1)S(1)}, u32[]{:S(2)}, u32[]{:S(2)}) async-start(bf16[8,64,256]{2,1,0:T(8,128)(2,1)} %bitcast.13), calls=%async_computation.2 | async-start | bytes 524288 | tf_op jit(solution)/shard_map/all_to_all | solution.py:587
  188.7 5.8 %fusion.78 = (bf16[1024,1024]{1,0:T(8,128)(2,1)S(1)}, f32[1024,1024]{1,0:T(8,128)}) fusion(bf16[1024,768]{1,0:T(8,128)(2,1)} %get-tuple-element.71, bf16[768,1536]{1,0:T(8,128)(2,1)} %all-gather.4.cloned.1.call-done), kind=kOutput, calls=%fused_computation.158 | convolution fusion | flops 1611661312 | bytes 9437184 | tf_op jit(solution)/shard_map/dot_general | solution.py:602
  195.4 1.1 collective-permute-start.12
  196.5 1.1 collective-permute-start.13
  197.6 1.3 collective-permute-start.14
  199.6 3.0 all-to-all-done.2
  203.5 28.7 %shard_map.291 = f32[64,2048]{1,0:T(8,128)} custom-call(s32[16,128]{1,0:T(8,128)} %reshape.283.seg_ref, bf16[128,128]{1,0:T(8,128)(2,1)} %fusion.50.flip_ref, bf16[64,16,128]{2,1,0:T(8,128)(2,1)} %reshape.262.x_ref, bf16[64,16,128]{2,1,0:T(8,128)(2,1)} %reshape.265.g_ref), custom_call_target="tpu_custom_call" | custom-call | flops 20000000000 | bytes 20000000 | tf_op jit(solution)/shard_map/pallas_call | solution.py:347
  232.2 2.0 copy.68
  234.1 17.1 %shard_map.290 = bf16[64,16,128]{2,1,0:T(8,128)(2,1)} custom-call(s32[16,128]{1,0:T(8,128)} %reshape.283.seg_ref, bf16[128,128]{1,0:T(8,128)(2,1)} %rev.3.flip_ref, bf16[64,16,128]{2,1,0:T(8,128)(2,1)} %reshape.265.g_ref, bf16[64,16,128,128]{3,2,1,0:T(8,128)(2,1)} %get-tuple-element.22.tt_ref), custom_call_target="tpu_custom_call" | custom-call | flops 15000000512 | bytes 15000000 | tf_op jit(solution)/shard_map/pallas_call | solution.py:273
  253.1 3.4 all-to-all-start.3
  256.6 15.4 %shard_map.292 = (f32[2,64,512]{2,1,0:T(8,128)}, f32[64,128]{1,0:T(8,128)}, f32[2,8,512]{2,1,0:T(8,128)}) custom-call(f32[1,512]{1,0:T(1,128)} %reshape.285.lam_log_ref, f32[1,512]{1,0:T(1,128)} %reshape.286.lam_freq_ref, f32[2,64,512]{2,1,0:T(8,128)} %convert_element_type.270.w_ref, f32[64,1]{1,0:T(8,128)} %copy.55.step_ref, f32[64,16,128]{2,1,0:T(8,128)} %bitcast.110, ...), custom_call_target="tpu_custom_call" | custom-call | flops 12000000000 | bytes 12000000 | tf_op jit(solution)/shard_map/pallas_call | solution.py:428
  273.7 3.8 %fusion.24 = (bf16[1024]{0:T(1024)(128)(2,1)S(1)}, f32[256]{0:T(256)S(1)}, f32[256]{0:T(256)S(1)}, bf16[1024]{0:T(1024)(128)(2,1)S(1)}, f32[256,1024]{1,0:T(8,128)}) fusion(bf16[256,1024]{1,0:T(8,128)(2,1)S(1)} %copy-done.2, f32[256]{0:T(256)S(1)} %add_rsqrt_fusion, f32[256]{0:T(256)S(1)} %broadcast_multiply_fusion.2, f32[1024]{0:T(1024)S(1)} %get-tuple-element.99, ...), kind=kOutput, calls=%fused_computation.45 | convolution fusion | flops 272889344 | bytes 5517312 | tf_op jit(solution)/shard_map/dot_general | solution.py:618
  278.2 1.2 pad_maximum_fusion.2
  287.9 2.3 convolution_convert_fusion.3
  290.2 3.0 convolution_convert_fusion.1
  293.3 1.6 pad_maximum_fusion
  294.9 5.7 %fusion.79 = (bf16[1024,1024]{1,0:T(8,128)(2,1)S(1)}, f32[1024,1024]{1,0:T(8,128)}) fusion(bf16[1024,768]{1,0:T(8,128)(2,1)} %copy-done.36, bf16[1024,768]{0,1:T(8,128)(2,1)} %all-gather.8.cloned.1.call-done), kind=kOutput, calls=%fused_computation.159 | convolution fusion | flops 1611661312 | bytes 9437184 | tf_op jit(solution)/shard_map/dot_general | solution.py:598
  301.0 1.3 collective-permute-start.24
  303.2 1.3 collective-permute-start.26
  304.5 1.2 fusion.69
  305.7 1.2 collective-permute-start.6
  307.9 1.3 collective-permute-start.8
  309.2 1.5 collective-permute-done.25
  315.7 6.1 %collective-permute-done.6 = bf16[256,1024]{1,0:T(8,128)(2,1)S(1)} collective-permute-done((bf16[256,1024]{1,0:T(8,128)(2,1)}, bf16[256,1024]{1,0:T(8,128)(2,1)S(1)}, u32[]{:S(2)}, u32[]{:S(2)}) %collective-permute-start.6) | collective-permute-done | bytes 524320 | tf_op jit(solution)/shard_map/ppermute | solution.py:466
  321.8 1.6 collective-permute-start.29
  323.4 9.8 %collective-permute-done.7 = bf16[256,1024]{1,0:T(8,128)(2,1)S(1)} collective-permute-done((bf16[256,1024]{1,0:T(8,128)(2,1)}, bf16[256,1024]{1,0:T(8,128)(2,1)S(1)}, u32[]{:S(2)}, u32[]{:S(2)}) %collective-permute-start.7) | collective-permute-done | bytes 524320 | tf_op jit(solution)/shard_map/ppermute | solution.py:466
  333.8 3.1 fusion.23
  339.0 1.5 collective-permute-start.20
  342.3 1.2 pad_maximum_fusion.6
  343.9 1.6 copy.66
  345.5 2.6 collective-permute-done.19
  349.7 1.4 collective-permute-start.21
  351.1 1.6 collective-permute-start.22
  355.1 4.7 %collective-permute-done.21 = bf16[96,1536]{1,0:T(8,128)(2,1)S(1)} collective-permute-done((bf16[96,1536]{1,0:T(8,128)(2,1)}, bf16[96,1536]{1,0:T(8,128)(2,1)S(1)}, u32[]{:S(2)}, u32[]{:S(2)}) %collective-permute-start.21) | collective-permute-done | bytes 294944 | tf_op jit(solution)/shard_map/ppermute | solution.py:466
  359.8 3.8 %collective-permute-done.22 = bf16[96,1536]{1,0:T(8,128)(2,1)S(1)} collective-permute-done((bf16[96,1536]{1,0:T(8,128)(2,1)}, bf16[96,1536]{1,0:T(8,128)(2,1)S(1)}, u32[]{:S(2)}, u32[]{:S(2)}) %collective-permute-start.22) | collective-permute-done | bytes 294944 | tf_op jit(solution)/shard_map/ppermute | solution.py:466
  364.7 1.1 pad_maximum_fusion.3
  366.4 1.3 slice.226
  (221 shorter events, 49.5 us)
Async XLA Ops:
  7.2 27.6 %copy-start = (bf16[384,1024]{1,0:T(8,128)(2,1)S(1)}, bf16[384,1024]{1,0:T(8,128)(2,1)}, u32[]{:S(2)}) copy-start(bf16[384,1024]{1,0:T(8,128)(2,1)} %param.21) | copy-start | bytes 2359300
  7.2 3.3 copy-start.23
  7.2 3.3 copy-start.24
  7.2 3.3 copy-start.21
  7.2 3.3 copy-start.25
  7.3 3.3 copy-start.26
  7.3 19.1 %copy-start.2 = (bf16[256,1024]{1,0:T(8,128)(2,1)S(1)}, bf16[256,1024]{1,0:T(8,128)(2,1)}, u32[]{:S(2)}) copy-start(bf16[256,1024]{1,0:T(8,128)(2,1)} %param.17) | copy-start | bytes 1572868
  7.3 62.9 %all-gather.6.cloned.1.call-start = ((), (), s32[]{:S(2)}) async-start(), calls=%async_computation.8 | async-start | bytes 1179648 | tf_op jit(solution)/shard_map/all_gather | solution.py:538
  8.0 129.9 %all-gather.8.cloned.1.call-start = ((), (), s32[]{:S(2)}) async-start(), calls=%async_computation.9 | async-start | bytes 1769472 | tf_op jit(solution)/shard_map/all_gather | solution.py:543
  8.1 22.3 %copy-start.5 = (bf16[256,1024]{1,0:T(8,128)(2,1)S(1)}, bf16[256,1024]{1,0:T(8,128)(2,1)}, u32[]{:S(2)}) copy-start(bf16[256,1024]{1,0:T(8,128)(2,1)} %param.33) | copy-start | bytes 1572868
  9.7 28.0 %copy-start.16 = (bf16[2,64,512]{2,1,0:T(8,128)(2,1)S(1)}, bf16[2,64,512]{2,1,0:T(8,128)(2,1)}, u32[]{:S(2)}) copy-start(bf16[2,64,512]{2,1,0:T(8,128)(2,1)} %param.27) | copy-start | bytes 393220
  10.4 146.3 %all-gather.4.cloned.1.call-start = ((), (), s32[]{:S(2)}) async-start(), calls=%async_computation.7 | async-start | bytes 2654208 | tf_op jit(solution)/shard_map/all_gather | solution.py:540
  27.3 131.9 %copy-start.3 = (bf16[256,1024]{1,0:T(8,128)(2,1)}, bf16[256,1024]{1,0:T(8,128)(2,1)S(1)}, u32[]{:S(2)}) copy-start(bf16[256,1024]{1,0:T(8,128)(2,1)S(1)} %fusion.19) | copy-start | bytes 1572868
  27.3 131.9 %collective-permute-start = (bf16[256,1024]{1,0:T(8,128)(2,1)S(1)}, bf16[256,1024]{1,0:T(8,128)(2,1)}, u32[]{:S(2)}, u32[]{:S(2)}) collective-permute-start(bf16[256,1024]{1,0:T(8,128)(2,1)S(1)} %fusion.19), channel_id=1, source_target_pairs={{0,8},{8,0},{16,24},{24,16},{1,9},{9,1},{17,25},{25,17},{2,10},{10... | collective-permute-start | bytes 1572872 | tf_op jit(solution)/shard_map/ppermute | solution.py:466
  28.8 130.3 %collective-permute-start.1 = (bf16[256,1024]{1,0:T(8,128)(2,1)S(1)}, bf16[256,1024]{1,0:T(8,128)(2,1)}, u32[]{:S(2)}, u32[]{:S(2)}) collective-permute-start(bf16[256,1024]{1,0:T(8,128)(2,1)S(1)} %fusion.19), channel_id=1, source_target_pairs={{0,16},{8,24},{16,0},{24,8},{1,17},{9,25},{17,1},{25,9},{2,18},{10... | collective-permute-start | bytes 1572872 | tf_op jit(solution)/shard_map/ppermute | solution.py:466
  30.4 89.3 %collective-permute-start.9 = (bf16[256,1024]{1,0:T(8,128)(2,1)S(1)}, bf16[256,1024]{1,0:T(8,128)(2,1)}, u32[]{:S(2)}, u32[]{:S(2)}) collective-permute-start(bf16[256,1024]{1,0:T(8,128)(2,1)S(1)} %copy-done.5), channel_id=1, source_target_pairs={{0,8},{8,0},{16,24},{24,16},{1,9},{9,1},{17,25},{25,17},{2,10},{10... | collective-permute-start | bytes 1572872 | tf_op jit(solution)/shard_map/ppermute | solution.py:466
  30.9 99.3 %collective-permute-start.10 = (bf16[256,1024]{1,0:T(8,128)(2,1)S(1)}, bf16[256,1024]{1,0:T(8,128)(2,1)S(1)}, u32[]{:S(2)}, u32[]{:S(2)}) collective-permute-start(bf16[256,1024]{1,0:T(8,128)(2,1)S(1)} %copy-done.5), channel_id=1, source_target_pairs={{0,16},{8,24},{16,0},{24,8},{1,17},{9,25},{17,1},{25,9},{2,18},{10... | collective-permute-start | bytes 1572872 | tf_op jit(solution)/shard_map/ppermute | solution.py:466
  31.4 101.0 %collective-permute-start.11 = (bf16[256,1024]{1,0:T(8,128)(2,1)S(1)}, bf16[256,1024]{1,0:T(8,128)(2,1)S(1)}, u32[]{:S(2)}, u32[]{:S(2)}) collective-permute-start(bf16[256,1024]{1,0:T(8,128)(2,1)S(1)} %copy-done.5), channel_id=1, source_target_pairs={{0,24},{8,16},{16,8},{24,0},{1,25},{9,17},{17,9},{25,1},{2,26},{10... | collective-permute-start | bytes 1572872 | tf_op jit(solution)/shard_map/ppermute | solution.py:466
  39.8 30.3 %copy-start.19 = (bf16[8,2048]{1,0:T(8,128)(2,1)S(1)}, bf16[8,2048]{1,0:T(8,128)(2,1)}, u32[]{:S(2)}) copy-start(bf16[8,2048]{1,0:T(8,128)(2,1)} %copy-done.18) | copy-start | bytes 98308
  73.6 21.5 %all-to-all-start = ((bf16[8,64,256]{2,1,0:T(8,128)(2,1)}), bf16[8,64,256]{2,1,0:T(8,128)(2,1)S(1)}, u32[]{:S(2)}, u32[]{:S(2)}) async-start(bf16[8,64,256]{2,1,0:T(8,128)(2,1)} %bitcast.4), calls=%async_computation | async-start | bytes 524288 | tf_op jit(solution)/shard_map/all_to_all | solution.py:569
  114.2 13.1 %all-to-all-start.1 = ((bf16[64,8,256]{2,0,1:T(8,128)(2,1)}), bf16[64,8,256]{2,0,1:T(8,128)(2,1)S(1)}, u32[]{:S(2)}, u32[]{:S(2)}) async-start(bf16[64,8,256]{2,0,1:T(8,128)(2,1)} %copy.56), calls=%async_computation.1 | async-start | bytes 524288 | tf_op jit(solution)/shard_map/all_to_all | solution.py:573
  117.6 194.9 %reduce-scatter.8.cloned.1.call-start = ((), (), s32[]{:S(2)}) async-start(), calls=%async_computation.12 | async-start | bytes 1769472 | tf_op jit(solution)/shard_map/reduce_scatter | solution.py:606
  127.3 29.5 %copy-start.12 = (bf16[64,8,256]{2,0,1:T(8,128)(2,1)}, bf16[64,8,256]{2,0,1:T(8,128)(2,1)S(1)}, u32[]{:S(2)}) copy-start(bf16[64,8,256]{2,0,1:T(8,128)(2,1)S(1)} %all-to-all-done.1) | copy-start | bytes 786436
  127.3 9.2 %collective-permute-start.3 = (bf16[512,256]{1,0:T(8,128)(2,1)S(1)}, bf16[512,256]{1,0:T(8,128)(2,1)S(1)}, u32[]{:S(2)}, u32[]{:S(2)}) collective-permute-start(bf16[512,256]{1,0:T(8,128)(2,1)S(1)} %bitcast.117), channel_id=1, source_target_pairs={{0,8},{8,0},{16,24},{24,16},{1,9},{9,1},{17,25},{25,17},{2,10},{10... | collective-permute-start | bytes 786440 | tf_op jit(solution)/shard_map/ppermute | solution.py:466
  130.1 29.0 %collective-permute-start.2 = (bf16[256,1024]{1,0:T(8,128)(2,1)S(1)}, bf16[256,1024]{1,0:T(8,128)(2,1)S(1)}, u32[]{:S(2)}, u32[]{:S(2)}) collective-permute-start(bf16[256,1024]{1,0:T(8,128)(2,1)S(1)} %fusion.19), channel_id=1, source_target_pairs={{0,24},{8,16},{16,8},{24,0},{1,25},{9,17},{17,9},{25,1},{2,26},{10... | collective-permute-start | bytes 1572872 | tf_op jit(solution)/shard_map/ppermute | solution.py:466
  133.2 23.5 %collective-permute-start.4 = (bf16[512,256]{1,0:T(8,128)(2,1)S(1)}, bf16[512,256]{1,0:T(8,128)(2,1)S(1)}, u32[]{:S(2)}, u32[]{:S(2)}) collective-permute-start(bf16[512,256]{1,0:T(8,128)(2,1)S(1)} %bitcast.118), channel_id=1, source_target_pairs={{0,16},{8,24},{16,0},{24,8},{1,17},{9,25},{17,1},{25,9},{2,18},{10... | collective-permute-start | bytes 786440 | tf_op jit(solution)/shard_map/ppermute | solution.py:466
  137.3 19.5 %collective-permute-start.5 = (bf16[512,256]{1,0:T(8,128)(2,1)S(1)}, bf16[512,256]{1,0:T(8,128)(2,1)S(1)}, u32[]{:S(2)}, u32[]{:S(2)}) collective-permute-start(bf16[512,256]{1,0:T(8,128)(2,1)S(1)} %bitcast.119), channel_id=1, source_target_pairs={{0,24},{8,16},{16,8},{24,0},{1,25},{9,17},{17,9},{25,1},{2,26},{10... | collective-permute-start | bytes 786440 | tf_op jit(solution)/shard_map/ppermute | solution.py:466
  137.9 18.8 %copy-start.32 = (bf16[512,256]{1,0:T(8,128)(2,1)S(1)}, bf16[512,256]{1,0:T(8,128)(2,1)}, u32[]{:S(2)}) copy-start(bf16[512,256]{1,0:T(8,128)(2,1)} %copy-done.31) | copy-start | bytes 786436
  159.8 7.7 %copy-start.29 = (bf16[256,1024]{1,0:T(8,128)(2,1)}, bf16[256,1024]{1,0:T(8,128)(2,1)S(1)}, u32[]{:S(2)}) copy-start(bf16[256,1024]{1,0:T(8,128)(2,1)S(1)} %collective-permute-done.2) | copy-start | bytes 1572868
  167.5 5.5 %copy-start.36 = (bf16[1024,768]{1,0:T(8,128)(2,1)}, bf16[1024,768]{1,0:T(8,128)(2,1)S(1)}, u32[]{:S(2)}) copy-start(bf16[1024,768]{1,0:T(8,128)(2,1)S(1)} %get-tuple-element.73) | copy-start | bytes 4718596
  167.5 5.5 %copy-start.17 = (bf16[1024,1024]{1,0:T(8,128)(2,1)S(1)}, bf16[1024,1024]{1,0:T(8,128)(2,1)}, u32[]{:S(2)}) copy-start(bf16[1024,1024]{1,0:T(8,128)(2,1)} %constant_dynamic-update-slice_fusion) | copy-start | bytes 6291460
  169.5 9.5 %collective-permute-start.15 = (bf16[512,256]{1,0:T(8,128)(2,1)}, bf16[512,256]{1,0:T(8,128)(2,1)S(1)}, u32[]{:S(2)}, u32[]{:S(2)}) collective-permute-start(bf16[512,256]{1,0:T(8,128)(2,1)} %get-tuple-element.86), channel_id=1, source_target_pairs={{0,8},{8,0},{16,24},{24,16},{1,9},{9,1},{17,25},{25,17},{2,10},{10... | collective-permute-start | bytes 786440 | tf_op jit(solution)/shard_map/ppermute | solution.py:466
  169.8 12.2 %collective-permute-start.16 = (bf16[512,256]{1,0:T(8,128)(2,1)}, bf16[512,256]{1,0:T(8,128)(2,1)S(1)}, u32[]{:S(2)}, u32[]{:S(2)}) collective-permute-start(bf16[512,256]{1,0:T(8,128)(2,1)} %get-tuple-element.88), channel_id=1, source_target_pairs={{0,16},{8,24},{16,0},{24,8},{1,17},{9,25},{17,1},{25,9},{2,18},{10... | collective-permute-start | bytes 786440 | tf_op jit(solution)/shard_map/ppermute | solution.py:466
  171.6 11.6 %collective-permute-start.17 = (bf16[512,256]{1,0:T(8,128)(2,1)S(1)}, bf16[512,256]{1,0:T(8,128)(2,1)}, u32[]{:S(2)}, u32[]{:S(2)}) collective-permute-start(bf16[512,256]{1,0:T(8,128)(2,1)S(1)} %get-tuple-element.87), channel_id=1, source_target_pairs={{0,24},{8,16},{16,8},{24,0},{1,25},{9,17},{17,9},{25,1},{2,26},{10... | collective-permute-start | bytes 786440 | tf_op jit(solution)/shard_map/ppermute | solution.py:466
  184.9 17.6 %all-to-all-start.2 = ((bf16[8,64,256]{2,1,0:T(8,128)(2,1)}), bf16[8,64,256]{2,1,0:T(8,128)(2,1)S(1)}, u32[]{:S(2)}, u32[]{:S(2)}) async-start(bf16[8,64,256]{2,1,0:T(8,128)(2,1)} %bitcast.13), calls=%async_computation.2 | async-start | bytes 524288 | tf_op jit(solution)/shard_map/all_to_all | solution.py:587
  195.4 78.3 %collective-permute-start.12 = (bf16[256,1024]{1,0:T(8,128)(2,1)}, bf16[256,1024]{1,0:T(8,128)(2,1)}, u32[]{:S(2)}, u32[]{:S(2)}) collective-permute-start(bf16[256,1024]{1,0:T(8,128)(2,1)} %get-tuple-element.76), channel_id=1, source_target_pairs={{0,8},{8,0},{16,24},{24,16},{1,9},{9,1},{17,25},{25,17},{2,10},{10... | collective-permute-start | bytes 1572872 | tf_op jit(solution)/shard_map/ppermute | solution.py:466
  196.5 77.2 %collective-permute-start.13 = (bf16[256,1024]{1,0:T(8,128)(2,1)S(1)}, bf16[256,1024]{1,0:T(8,128)(2,1)}, u32[]{:S(2)}, u32[]{:S(2)}) collective-permute-start(bf16[256,1024]{1,0:T(8,128)(2,1)S(1)} %get-tuple-element.78), channel_id=1, source_target_pairs={{0,16},{8,24},{16,0},{24,8},{1,17},{9,25},{17,1},{25,9},{2,18},{10... | collective-permute-start | bytes 1572872 | tf_op jit(solution)/shard_map/ppermute | solution.py:466
  197.6 76.1 %collective-permute-start.14 = (bf16[256,1024]{1,0:T(8,128)(2,1)S(1)}, bf16[256,1024]{1,0:T(8,128)(2,1)}, u32[]{:S(2)}, u32[]{:S(2)}) collective-permute-start(bf16[256,1024]{1,0:T(8,128)(2,1)S(1)} %get-tuple-element.77), channel_id=1, source_target_pairs={{0,24},{8,16},{16,8},{24,0},{1,25},{9,17},{17,9},{25,1},{2,26},{10... | collective-permute-start | bytes 1572872 | tf_op jit(solution)/shard_map/ppermute | solution.py:466
  253.1 19.9 %all-to-all-start.3 = ((bf16[64,8,256]{2,0,1:T(8,128)(2,1)}), bf16[64,8,256]{2,0,1:T(8,128)(2,1)S(1)}, u32[]{:S(2)}, u32[]{:S(2)}) async-start(bf16[64,8,256]{2,0,1:T(8,128)(2,1)} %copy.59), calls=%async_computation.3 | async-start | bytes 524288 | tf_op jit(solution)/shard_map/all_to_all | solution.py:590
  256.5 80.5 %reduce-scatter.4.cloned.1.call-start = ((), (), s32[]{:S(2)}) async-start(), calls=%async_computation.10 | async-start | bytes 1327104 | tf_op jit(solution)/shard_map/reduce_scatter | solution.py:644
  273.7 4.0 %copy-start.4 = (bf16[256,1024]{1,0:T(8,128)(2,1)S(1)}, bf16[256,1024]{1,0:T(8,128)(2,1)}, u32[]{:S(2)}) copy-start(bf16[256,1024]{1,0:T(8,128)(2,1)} %copy-done.3) | copy-start | bytes 1572868
  278.2 9.7 %copy-start.8 = (bf16[1024,768]{1,0:T(8,128)(2,1)S(1)}, bf16[1024,768]{1,0:T(8,128)(2,1)}, u32[]{:S(2)}) copy-start(bf16[1024,768]{1,0:T(8,128)(2,1)} %copy-done.7) | copy-start | bytes 4718596
  278.2 9.7 %copy-start.13 = (bf16[64,8,256]{2,0,1:T(8,128)(2,1)S(1)}, bf16[64,8,256]{2,0,1:T(8,128)(2,1)}, u32[]{:S(2)}) copy-start(bf16[64,8,256]{2,0,1:T(8,128)(2,1)} %copy-done.12) | copy-start | bytes 786436
  279.4 70.2 %reduce-scatter.6.cloned.1.call-start = ((), (), s32[]{:S(2)}) async-start(), calls=%async_computation.11 | async-start | bytes 2654208 | tf_op jit(solution)/shard_map/reduce_scatter | solution.py:606
  294.9 5.7 %copy-start.11 = (f32[2,64,512]{2,1,0:T(8,128)S(1)}, f32[2,64,512]{2,1,0:T(8,128)}, u32[]{:S(2)}) copy-start(f32[2,64,512]{2,1,0:T(8,128)} %get-tuple-element.26) | copy-start | bytes 786436
  294.9 5.8 %copy-start.20 = (f32[64,128]{1,0:T(8,128)S(1)}, f32[64,128]{1,0:T(8,128)}, u32[]{:S(2)}) copy-start(f32[64,128]{1,0:T(8,128)} %get-tuple-element.27) | copy-start | bytes 98308
  301.0 6.9 %collective-permute-start.24 = (bf16[129,512]{1,0:T(8,128)(2,1)S(1)}, bf16[129,512]{1,0:T(8,128)(2,1)S(1)}, u32[]{:S(2)}, u32[]{:S(2)}) collective-permute-start(bf16[129,512]{1,0:T(8,128)(2,1)S(1)} %convert_element_type.310), channel_id=1, source_target_pairs={{0,8},{8,0},{16,24},{24,16},{1,9},{9,1},{17,25},{25,17},{2,10},{10... | collective-permute-start | bytes 396296 | tf_op jit(solution)/shard_map/ppermute | solution.py:466
  302.2 8.5 %collective-permute-start.25 = (bf16[129,512]{1,0:T(8,128)(2,1)S(1)}, bf16[129,512]{1,0:T(8,128)(2,1)S(1)}, u32[]{:S(2)}, u32[]{:S(2)}) collective-permute-start(bf16[129,512]{1,0:T(8,128)(2,1)S(1)} %convert_element_type.310), channel_id=1, source_target_pairs={{0,16},{8,24},{16,0},{24,8},{1,17},{9,25},{17,1},{25,9},{2,18},{10... | collective-permute-start | bytes 396296 | tf_op jit(solution)/shard_map/ppermute | solution.py:466
  303.2 8.0 %collective-permute-start.26 = (bf16[129,512]{1,0:T(8,128)(2,1)S(1)}, bf16[129,512]{1,0:T(8,128)(2,1)S(1)}, u32[]{:S(2)}, u32[]{:S(2)}) collective-permute-start(bf16[129,512]{1,0:T(8,128)(2,1)S(1)} %convert_element_type.310), channel_id=1, source_target_pairs={{0,24},{8,16},{16,8},{24,0},{1,25},{9,17},{17,9},{25,1},{2,26},{10... | collective-permute-start | bytes 396296 | tf_op jit(solution)/shard_map/ppermute | solution.py:466
  304.5 29.3 %copy-start.6 = (bf16[256,1024]{1,0:T(8,128)(2,1)S(1)}, bf16[256,1024]{1,0:T(8,128)(2,1)}, u32[]{:S(2)}) copy-start(bf16[256,1024]{1,0:T(8,128)(2,1)} %param.33) | copy-start | bytes 1572868
  305.7 28.1 %copy-start.9 = (f32[256,1024]{1,0:T(8,128)S(1)}, f32[256,1024]{1,0:T(8,128)}, u32[]{:S(2)}) copy-start(f32[256,1024]{1,0:T(8,128)} %get-tuple-element.72) | copy-start | bytes 3145732
  305.7 16.1 %collective-permute-start.6 = (bf16[256,1024]{1,0:T(8,128)(2,1)}, bf16[256,1024]{1,0:T(8,128)(2,1)S(1)}, u32[]{:S(2)}, u32[]{:S(2)}) collective-permute-start(bf16[256,1024]{1,0:T(8,128)(2,1)} %get-tuple-element.79), channel_id=1, source_target_pairs={{0,8},{8,0},{16,24},{24,16},{1,9},{9,1},{17,25},{25,17},{2,10},{10... | collective-permute-start | bytes 1572872 | tf_op jit(solution)/shard_map/ppermute | solution.py:466
  306.9 26.3 %collective-permute-start.7 = (bf16[256,1024]{1,0:T(8,128)(2,1)}, bf16[256,1024]{1,0:T(8,128)(2,1)S(1)}, u32[]{:S(2)}, u32[]{:S(2)}) collective-permute-start(bf16[256,1024]{1,0:T(8,128)(2,1)} %get-tuple-element.81), channel_id=1, source_target_pairs={{0,16},{8,24},{16,0},{24,8},{1,17},{9,25},{17,1},{25,9},{2,18},{10... | collective-permute-start | bytes 1572872 | tf_op jit(solution)/shard_map/ppermute | solution.py:466
  307.9 26.0 %collective-permute-start.8 = (bf16[256,1024]{1,0:T(8,128)(2,1)}, bf16[256,1024]{1,0:T(8,128)(2,1)}, u32[]{:S(2)}, u32[]{:S(2)}) collective-permute-start(bf16[256,1024]{1,0:T(8,128)(2,1)} %get-tuple-element.80), channel_id=1, source_target_pairs={{0,24},{8,16},{16,8},{24,0},{1,25},{9,17},{17,9},{25,1},{2,26},{10... | collective-permute-start | bytes 1572872 | tf_op jit(solution)/shard_map/ppermute | solution.py:466
  313.6 25.4 %collective-permute-start.27 = (bf16[128,8,96]{0,2,1:T(8,128)(2,1)S(1)}, bf16[128,8,96]{0,2,1:T(8,128)(2,1)}, u32[]{:S(2)}, u32[]{:S(2)}) collective-permute-start(bf16[128,8,96]{0,2,1:T(8,128)(2,1)S(1)} %bitcast.104), channel_id=1, source_target_pairs={{0,8},{8,0},{16,24},{24,16},{1,9},{9,1},{17,25},{25,17},{2,10},{10... | collective-permute-start | bytes 589832 | tf_op jit(solution)/shard_map/ppermute | solution.py:466
  314.6 26.8 %collective-permute-start.28 = (bf16[128,8,96]{0,2,1:T(8,128)(2,1)S(1)}, bf16[128,8,96]{0,2,1:T(8,128)(2,1)}, u32[]{:S(2)}, u32[]{:S(2)}) collective-permute-start(bf16[128,8,96]{0,2,1:T(8,128)(2,1)S(1)} %bitcast.105), channel_id=1, source_target_pairs={{0,16},{8,24},{16,0},{24,8},{1,17},{9,25},{17,1},{25,9},{2,18},{10... | collective-permute-start | bytes 589832 | tf_op jit(solution)/shard_map/ppermute | solution.py:466
  321.8 20.5 %collective-permute-start.29 = (bf16[128,8,96]{0,2,1:T(8,128)(2,1)S(1)}, bf16[128,8,96]{0,2,1:T(8,128)(2,1)}, u32[]{:S(2)}, u32[]{:S(2)}) collective-permute-start(bf16[128,8,96]{0,2,1:T(8,128)(2,1)S(1)} %bitcast.106), channel_id=1, source_target_pairs={{0,24},{8,16},{16,8},{24,0},{1,25},{9,17},{17,9},{25,1},{2,26},{10... | collective-permute-start | bytes 589832 | tf_op jit(solution)/shard_map/ppermute | solution.py:466
  337.0 8.5 %collective-permute-start.18 = (bf16[66,1024]{1,0:T(8,128)(2,1)}, bf16[66,1024]{1,0:T(8,128)(2,1)S(1)}, u32[]{:S(2)}, u32[]{:S(2)}) collective-permute-start(bf16[66,1024]{1,0:T(8,128)(2,1)} %bitcast.123), channel_id=1, source_target_pairs={{0,8},{8,0},{16,24},{24,16},{1,9},{9,1},{17,25},{25,17},{2,10},{10... | collective-permute-start | bytes 405512 | tf_op jit(solution)/shard_map/ppermute | solution.py:466
  337.9 10.2 %collective-permute-start.19 = (bf16[66,1024]{1,0:T(8,128)(2,1)}, bf16[66,1024]{1,0:T(8,128)(2,1)S(1)}, u32[]{:S(2)}, u32[]{:S(2)}) collective-permute-start(bf16[66,1024]{1,0:T(8,128)(2,1)} %bitcast.124), channel_id=1, source_target_pairs={{0,16},{8,24},{16,0},{24,8},{1,17},{9,25},{17,1},{25,9},{2,18},{10... | collective-permute-start | bytes 405512 | tf_op jit(solution)/shard_map/ppermute | solution.py:466
  339.0 9.1 %collective-permute-start.20 = (bf16[66,1024]{1,0:T(8,128)(2,1)}, bf16[66,1024]{1,0:T(8,128)(2,1)S(1)}, u32[]{:S(2)}, u32[]{:S(2)}) collective-permute-start(bf16[66,1024]{1,0:T(8,128)(2,1)} %bitcast.125), channel_id=1, source_target_pairs={{0,24},{8,16},{16,8},{24,0},{1,25},{9,17},{17,9},{25,1},{2,26},{10... | collective-permute-start | bytes 405512 | tf_op jit(solution)/shard_map/ppermute | solution.py:466
  343.9 4.2 %copy-start.15 = (bf16[1,66,1024]{2,1,0:T(8,128)(2,1)S(1)}, bf16[1,66,1024]{2,1,0:T(8,128)(2,1)}, u32[]{:S(2)}) copy-start(bf16[1,66,1024]{2,1,0:T(8,128)(2,1)} %reduce-scatter.4.cloned.1.call-done) | copy-start | bytes 405508
  349.7 10.2 %collective-permute-start.21 = (bf16[96,1536]{1,0:T(8,128)(2,1)}, bf16[96,1536]{1,0:T(8,128)(2,1)S(1)}, u32[]{:S(2)}, u32[]{:S(2)}) collective-permute-start(bf16[96,1536]{1,0:T(8,128)(2,1)} %reduce-scatter.6.cloned.1.call-done), channel_id=1, source_target_pairs={{0,8},{8,0},{16,24},{24,16},{1,9},{9,1},{17,25},{25,17},{2,10},{10... | collective-permute-start | bytes 884744 | tf_op jit(solution)/shard_map/ppermute | solution.py:466
  351.1 12.5 %collective-permute-start.22 = (bf16[96,1536]{1,0:T(8,128)(2,1)}, bf16[96,1536]{1,0:T(8,128)(2,1)S(1)}, u32[]{:S(2)}, u32[]{:S(2)}) collective-permute-start(bf16[96,1536]{1,0:T(8,128)(2,1)} %reduce-scatter.6.cloned.1.call-done), channel_id=1, source_target_pairs={{0,16},{8,24},{16,0},{24,8},{1,17},{9,25},{17,1},{25,9},{2,18},{10... | collective-permute-start | bytes 884744 | tf_op jit(solution)/shard_map/ppermute | solution.py:466
  352.7 12.0 %collective-permute-start.23 = (bf16[96,1536]{1,0:T(8,128)(2,1)}, bf16[96,1536]{1,0:T(8,128)(2,1)S(1)}, u32[]{:S(2)}, u32[]{:S(2)}) collective-permute-start(bf16[96,1536]{1,0:T(8,128)(2,1)} %reduce-scatter.6.cloned.1.call-done), channel_id=1, source_target_pairs={{0,24},{8,16},{16,8},{24,0},{1,25},{9,17},{17,9},{25,1},{2,26},{10... | collective-permute-start | bytes 884744 | tf_op jit(solution)/shard_map/ppermute | solution.py:466
  (15 other events, 34.3 us)
Sparse Core Ops, SparseCore 0:
  9.7 24.8 all-gather.5
  36.8 26.9 all-gather.7
  66.0 36.3 all-gather.3
  176.3 34.5 reduce-scatter.7
  279.6 33.0 reduce-scatter.3
  314.9 34.7 reduce-scatter.5
